TPU v7x, 32 devices: a whole 2x2x4 slice. The times are simulated.
32 devices in a mesh: seq: 8 (over z, y), head: 4 (over x, core).
Axes of the slice: x: 2, y: 2, z: 4, core: 2. Of those that a mesh axis runs over, the one named last changes fastest.
Arguments:
- queries: bfloat16 [2048, 4096], P('seq', 'head'), may hold values from -140 to 140
- key_rows: bfloat16 [2048, 1024], P('seq', 'head'), may hold values from -15 to 15
- value_rows: bfloat16 [2048, 1024], P('seq', 'head'), may hold values from -4.5 to 4.5
- span_place: int32 [16], replicated, may hold values from 0 to 15, as said below
- block_lists: int32 [16, 3], replicated, may hold values from 0 to 14, as said below
- cotangent: bfloat16 [2048, 4096], P(('seq', 'head')), may hold values from -4.5 to 4.5
Outputs:
- attended: bfloat16 [2048, 4096], P(('seq', 'head'))
- query_grad: bfloat16 [2048, 4096], P('seq', 'head')
- key_grad: bfloat16 [2048, 1024], P('seq', 'head')
- value_grad: bfloat16 [2048, 1024], P('seq', 'head')
Inputs may be any that keep to these rules, and one draw needn't show every extreme that they name: `span_place`: storage slots 2i and 2i+1 hold blocks c and 15 - c for some c below 8; each block is held once. `block_lists`: call blocks c and 15 - c a pair. Each entry of row b is an earlier block or b itself. Among the entries of the two rows of one pair, those that are not their own row's block lie in distinct pairs, none of them that pair.
All inputs are finite; a program needn't handle non-finite values.
Results may differ from a plain program's by a relative error of at most 0.035.
Values may be sent and summed in bfloat16 or wider, within the bound.
A program may use at most 64 MiB of HBM per device.

v0:
```python
import math

import jax
import jax.numpy as jnp
from jax import lax
from jax.sharding import PartitionSpec as P

HEAD_DIM = 128


def lookup(lookup_table, selector, table_rows):
    matches = selector[..., None] == jnp.arange(table_rows, dtype=jnp.int32)
    return jnp.sum(jnp.where(matches[..., None], lookup_table, 0), axis=-2)


def block_layout(span_place, block_lists):
    slot_total = span_place.shape[0]
    slot_ids = jnp.arange(slot_total, dtype=jnp.int32)
    slot_of = jnp.sum(
        jnp.where(span_place[:, None] == slot_ids[None, :], slot_ids[:, None], 0), axis=0
    )
    pick_blocks = lookup(block_lists, span_place, slot_total)
    valid_cols = []
    for column in range(pick_blocks.shape[1]):
        kept_pick = pick_blocks[:, column] != span_place
        for before in range(column):
            kept_pick = kept_pick & (pick_blocks[:, column] != pick_blocks[:, before])
        valid_cols.append(kept_pick)
    pick_valid = jnp.stack(valid_cols, axis=1)
    pick_slots = lookup(slot_of[:, None], pick_blocks, slot_total)[..., 0]
    return (pick_slots, pick_valid)


def attend_block(query_block, key_set, value_set, grad_block, visible_picks, score_scale):
    span_rows = query_block.shape[0]
    set_count = key_set.shape[0]
    scores = (
        jnp.einsum("ckgd,jekd->kgcje", query_block, key_set, preferred_element_type=jnp.float32)
        * score_scale
    )
    causal = jnp.arange(span_rows)[None, :] <= jnp.arange(span_rows)[:, None]
    others = jnp.broadcast_to(visible_picks[None, :, None], (span_rows, set_count - 1, span_rows))
    allowed = jnp.concatenate([causal[:, None, :], others], axis=1)
    scores = jnp.where(allowed, scores, -jnp.inf)
    row_top = jnp.max(scores, axis=(3, 4), keepdims=True)
    row_total = jnp.sum(jnp.exp(scores - row_top), axis=(3, 4), keepdims=True)
    log_total = row_top + jnp.log(row_total)
    probabilities = jnp.exp(scores - log_total)
    weights = probabilities.astype(jnp.bfloat16)
    attended = jnp.einsum(
        "kgcje,jekd->ckgd", weights, value_set, preferred_element_type=jnp.float32
    ).astype(jnp.bfloat16)
    attended_wide = lax.optimization_barrier(attended).astype(jnp.float32)
    row_delta = jnp.sum(grad_block.astype(jnp.float32) * attended_wide, axis=-1)
    slopes = jnp.einsum(
        "ckgd,jekd->kgcje", grad_block, value_set, preferred_element_type=jnp.float32
    )
    shifted = slopes - jnp.transpose(row_delta, (1, 2, 0))[..., None, None]
    dscores = (probabilities * shifted * score_scale).astype(jnp.bfloat16)
    query_grad = jnp.einsum(
        "kgcje,jekd->ckgd", dscores, key_set, preferred_element_type=jnp.float32
    ).astype(jnp.bfloat16)
    key_part = jnp.einsum(
        "kgcje,ckgd->jekd", dscores, query_block, preferred_element_type=jnp.float32
    )
    value_part = jnp.einsum(
        "kgcje,ckgd->jekd", weights, grad_block, preferred_element_type=jnp.float32
    )
    return (attended, query_grad, key_part, value_part)


def body(queries, key_rows, value_rows, span_place, block_lists, cotangent):
    seq_count = lax.axis_size("seq")
    seq_index = lax.axis_index("seq")
    slot_total = span_place.shape[0]
    pick_count = block_lists.shape[1]
    span_rows = queries.shape[0] // 2
    kv_local = key_rows.shape[1] // HEAD_DIM
    group_size = queries.shape[1] // HEAD_DIM // kv_local
    kv_width = key_rows.shape[1]
    score_scale = 1.0 / math.sqrt(HEAD_DIM)
    grad_heads = lax.all_to_all(cotangent, "head", split_axis=1, concat_axis=0, tiled=True)
    pick_slots, pick_valid = block_layout(span_place, block_lists)
    owners = pick_slots // 2
    halves = pick_slots % 2
    req_owner = owners.reshape(seq_count, 2 * pick_count)
    req_half = halves.reshape(seq_count, 2 * pick_count)
    req_valid = pick_valid.reshape(seq_count, 2 * pick_count)
    served = req_valid & (req_owner == seq_index)
    paired = jnp.concatenate([key_rows, value_rows], axis=1)
    local_pair = paired.reshape(2, span_rows, 2 * kv_width)
    own_slots = seq_index * 2 + jnp.arange(2, dtype=jnp.int32)
    my_slots = lookup(pick_slots, own_slots, slot_total)
    my_valid = lookup(pick_valid.astype(jnp.int32), own_slots, slot_total) > 0
    my_owner = (my_slots // 2).reshape(-1)
    starts = my_slots.reshape(-1) * span_rows
    blank_set = jnp.zeros((2 * pick_count, span_rows, 2 * kv_width), paired.dtype)
    shard_part = lax.all_gather(paired, "seq", axis=0, tiled=True)
    piece_rows = shard_part.shape[0]
    row_index = starts[:, None] + jnp.arange(span_rows, dtype=jnp.int32)[None, :]
    inside = (row_index >= 0) & (row_index < piece_rows)
    taken_rows = jnp.take(shard_part, jnp.clip(row_index, 0, piece_rows - 1).reshape(-1), axis=0)
    fetched = jnp.where(inside[:, :, None], taken_rows.reshape(blank_set.shape), blank_set)
    fetched = fetched.reshape(2, pick_count, span_rows, 2 * kv_width)
    query_sets = queries.reshape(2, span_rows, kv_local, group_size, HEAD_DIM)
    grad_sets = grad_heads.reshape(2, span_rows, kv_local, group_size, HEAD_DIM)
    outputs = []
    query_grads = []
    own_parts = []
    sent_parts = []
    for which_half in range(2):
        key_set = jnp.concatenate([local_pair[which_half][None], fetched[which_half]], axis=0)
        keys_here = key_set[:, :, :kv_width].reshape(pick_count + 1, span_rows, kv_local, HEAD_DIM)
        values_here = key_set[:, :, kv_width:].reshape(
            pick_count + 1, span_rows, kv_local, HEAD_DIM
        )
        attended, query_grad, key_part, value_part = attend_block(
            query_sets[which_half],
            keys_here,
            values_here,
            grad_sets[which_half],
            my_valid[which_half],
            score_scale,
        )
        outputs.append(attended)
        query_grads.append(query_grad)
        grad_parts = jnp.concatenate(
            [
                key_part.reshape(pick_count + 1, span_rows, kv_width),
                value_part.reshape(pick_count + 1, span_rows, kv_width),
            ],
            axis=2,
        )
        own_parts.append(grad_parts[0])
        sent_parts.append(grad_parts[1:].astype(jnp.bfloat16))
    outgoing_grads = jnp.concatenate(sent_parts, axis=0)
    routing = (
        (my_owner[None, :] == jnp.arange(seq_count, dtype=jnp.int32)[:, None])
        & my_valid.reshape(-1)[None, :]
    ).astype(jnp.bfloat16)
    bundle = jnp.einsum(
        "op,pcw->ocw", routing, outgoing_grads, preferred_element_type=jnp.float32
    ).astype(jnp.bfloat16)
    returned = lax.all_to_all(bundle, "seq", split_axis=0, concat_axis=0, tiled=True)
    take_half = jnp.stack([jnp.any(served & (req_half == side), axis=1) for side in range(2)])
    gathered = jnp.einsum(
        "hr,rcw->hcw", take_half.astype(jnp.bfloat16), returned, preferred_element_type=jnp.float32
    )
    totals = jnp.stack(own_parts) + gathered
    key_grad = totals[:, :, :kv_width].reshape(2 * span_rows, kv_width).astype(jnp.bfloat16)
    value_grad = totals[:, :, kv_width:].reshape(2 * span_rows, kv_width).astype(jnp.bfloat16)
    attended_all = jnp.stack(outputs).reshape(2 * span_rows, queries.shape[1])
    query_grad_all = jnp.stack(query_grads).reshape(2 * span_rows, queries.shape[1])
    attended_out = lax.all_to_all(attended_all, "head", split_axis=0, concat_axis=1, tiled=True)
    return (attended_out, query_grad_all, key_grad, value_grad)


def solution(mesh):
    in_specs = (
        P("seq", "head"),
        P("seq", "head"),
        P("seq", "head"),
        P(),
        P(),
        P(("seq", "head"), None),
    )
    out_specs = (P(("seq", "head"), None), P("seq", "head"), P("seq", "head"), P("seq", "head"))
    return jax.shard_map(body, mesh=mesh, in_specs=in_specs, out_specs=out_specs, check_vma=False)
```

profile of v0, /device:TPU:0, one launch (start us, length us, event | category | flops | bytes accessed | tf_op | source)
XLA Modules:
  0.0 135.2 jit_solution(1251177123511875734)
XLA Ops:
  7.2 1.0 constant_dynamic-update-slice_fusion.1
  8.2 0.9 constant_dynamic-update-slice_fusion
  9.1 0.7 copy-done.9
  9.9 1.9 %copy.321 = bf16[8,4,8,1024]{3,2,0,1:T(8,128)(2,1)} copy(bf16[8,4,8,1024]{3,2,1,0:T(8,128)(2,1)} %bitcast.206) | data formatting | bytes 1048576 | tf_op jit(solution)/shard_map/all_to_all | solution.py:82
  11.8 4.2 %all-to-all-start.1 = ((bf16[64,4,1024]{2,0,1:T(8,128)(2,1)}), bf16[64,4,1024]{2,0,1:T(8,128)(2,1)S(1)}, u32[]{:S(2)}, u32[]{:S(2)}) async-start(bf16[64,4,1024]{2,0,1:T(8,128)(2,1)} %bitcast.175), calls=%async_computation.1 | async-start | bytes 1048576 | tf_op jit(solution)/shard_map/all_to_all | solution.py:82
  18.1 0.9 copy.284
  19.3 5.6 %all-to-all-done.1 = bf16[64,4,1024]{2,0,1:T(8,128)(2,1)S(1)} async-done(((bf16[64,4,1024]{2,0,1:T(8,128)(2,1)}), bf16[64,4,1024]{2,0,1:T(8,128)(2,1)S(1)}, u32[]{:S(2)}, u32[]{:S(2)}) %all-to-all-start.1) | async-done | bytes 524320 | tf_op jit(solution)/shard_map/all_to_all | solution.py:82
  25.1 0.9 copy.192
  26.0 0.9 copy.244
  27.5 35.4 %all-gather.2.cloned.1.call-done = bf16[2048,512]{1,0:T(8,128)(2,1)} async-done(((bf16[256,512]{1,0:T(8,128)(2,1)}), bf16[2048,512]{1,0:T(8,128)(2,1)}) %all-gather.2.cloned.1.call-update) | async-done | bytes 2097168 | tf_op jit(solution)/shard_map/all_gather | solution.py:98
  62.9 4.6 %gather_fusion = bf16[768,512]{1,0:T(8,128)(2,1)S(1)} fusion(bf16[2048,512]{1,0:T(8,128)(2,1)} %all-gather.2.cloned.1.call-done, s32[1024]{0:T(1024)S(1)} %pad_clamp_fusion), kind=kCustom, calls=%fused_computation | custom fusion | bytes 1575936 | tf_op jit(solution)/shard_map/jit(_take)/gather | solution.py:102
  67.5 0.4 copy.174
  68.0 0.8 fusion.25
  68.8 0.5 fusion.63
  69.3 0.3 exponential_reduce_fusion
  69.7 0.5 fusion.9
  70.2 0.5 convolution_bitcast_fusion
  70.8 0.7 fusion.2
  71.5 0.5 convolution_bitcast_fusion.1
  72.0 0.5 copy-done
  72.7 0.2 copy.214
  73.0 1.5 %fusion.64 = (f32[2,4,128]{2,1,0:T(4,128)S(1)}, f32[2,4,128,4,128]{2,4,1,3,0:T(8,128)S(1)}) fusion(bf16[128,2,4,128,1]{0,3,2,4,1:T(8,128)(2,1)} %bitcast.193, bf16[4,128,2,128,1]{1,3,2,0,4:T(8,128)(2,1)} %bitcast.202, pred[128,4,128]{0,2,1:T(8,128)(4,1)S(1)} %get-tuple-element.24), kind=kOutput, calls=%fused_computation.145 | convolution fusion | flops 135789568 | bytes 2691072 | tf_op jit(solution)/shard_map/ckgd,jekd->kgcje/dot_general | solution.py:38
  74.5 0.3 exponential_reduce_fusion.1
  74.8 0.5 fusion.8
  75.4 0.7 copy-done.6
  76.1 0.8 pad_maximum_fusion.2
  76.9 2.1 %copy.187 = bf16[2,128,2,4,128]{4,3,2,1,0:T(4,128)(2,1)} copy(bf16[2,128,2,4,128]{1,4,3,2,0:T(8,128)(2,1)} %pad_maximum_fusion.2) | data formatting | bytes 1048576 | tf_op jit(solution)/shard_map/stack | solution.py:152
  79.0 2.2 %all_to_all.29 = bf16[4,64,1024]{2,1,0:T(8,128)(2,1)} reshape(bf16[2,128,2,4,128]{4,3,2,1,0:T(4,128)(2,1)} %copy.187) | data formatting | bytes 1048576 | tf_op jit(solution)/shard_map/all_to_all | solution.py:154
  81.2 4.3 %all-to-all-start = ((bf16[4,64,1024]{2,1,0:T(8,128)(2,1)}), bf16[4,64,1024]{2,1,0:T(8,128)(2,1)}, u32[]{:S(2)}, u32[]{:S(2)}) async-start(bf16[4,64,1024]{2,1,0:T(8,128)(2,1)} %all_to_all.29), calls=%async_computation | async-start | bytes 1048576 | tf_op jit(solution)/shard_map/all_to_all | solution.py:154
  85.6 2.3 %convolution_bitcast_fusion.2 = f32[4,128,2,128]{1,3,0,2:T(8,128)} fusion(bf16[128,2,4,128,1]{0,3,2,4,1:T(8,128)(2,1)} %copy.244, f32[2,4,128,4,128]{2,4,1,3,0:T(8,128)S(1)} %get-tuple-element.38, f32[2,4,128]{2,1,0:T(4,128)S(1)} %bitcast.211), kind=kOutput, calls=%fused_computation.21 | convolution fusion | flops 135266304 | bytes 2887680 | tf_op jit(solution)/shard_map/kgcje,ckgd->jekd/dot_general | solution.py:66
  88.0 0.7 fusion.5
  88.8 0.5 convolution_bitcast_fusion.3
  89.3 0.3 fusion.15
  90.0 1.1 copy.205
  91.4 0.3 fusion.16
  91.7 0.6 convolution_convert_fusion
  92.4 1.3 copy.216
  93.7 0.6 all-to-all-done
  94.3 4.2 %all-to-all-start.2 = ((bf16[8,128,512]{2,1,0:T(8,128)(2,1)}), bf16[8,128,512]{2,1,0:T(8,128)(2,1)}, u32[]{:S(2)}, u32[]{:S(2)}) async-start(bf16[8,128,512]{2,1,0:T(8,128)(2,1)} %copy.216), calls=%async_computation.2 | async-start | bytes 2097152 | tf_op jit(solution)/shard_map/all_to_all | solution.py:144
  99.0 1.3 fusion.13
  100.2 1.5 %fusion.14 = bf16[1,128,2,4,128]{1,4,3,2,0:T(8,128)(2,1)S(1)} fusion(bf16[2,4,128,4,128]{2,4,1,3,0:T(8,128)(2,1)} %copy-done.2, bf16[4,128,2,128,1]{1,3,2,0,4:T(8,128)(2,1)S(1)} %bitcast.203), kind=kOutput, calls=%fused_computation.33 | convolution fusion | flops 134348800 | bytes 1572864 | tf_op jit(solution)/shard_map/kgcje,jekd->ckgd/dot_general | solution.py:60
  101.8 0.3 copy.200
  102.2 1.2 reshape.297
  103.8 1.9 %copy.287 = bf16[4,8,8,1024]{3,2,0,1:T(8,128)(2,1)} copy(bf16[4,8,8,1024]{3,2,1,0:T(8,128)(2,1)} %bitcast.101) | data formatting | bytes 1048576 | tf_op jit(solution)/shard_map/all_to_all | solution.py:154
  105.7 18.8 %all-to-all-done.2 = bf16[8,128,512]{2,1,0:T(8,128)(2,1)} async-done(((bf16[8,128,512]{2,1,0:T(8,128)(2,1)}), bf16[8,128,512]{2,1,0:T(8,128)(2,1)}, u32[]{:S(2)}, u32[]{:S(2)}) %all-to-all-start.2) | async-done | bytes 1048608 | tf_op jit(solution)/shard_map/all_to_all | solution.py:144
  124.5 2.3 %fusion.12 = bf16[2,128,512]{2,0,1:T(2,128)(2,1)S(1)} fusion(bf16[8,128,512]{2,1,0:T(8,128)(2,1)} %all-to-all-done.2, f32[1,128,512]{2,0,1:T(1,128)S(1)} %fusion.27, f32[1,128,512]{2,0,1:T(1,128)S(1)} %fusion.28, pred[1,8]{1,0:T(4,128)(4,1)S(1)} %bitcast.223, pred[1,8]{1,0:T(4,128)(4,1)S(1)} %bitcast.222), kind=kOutput, calls=%fused_computation.31 | convolution fusion | flops 2490384 | bytes 1835024 | tf_op jit(solution)/shard_map/hr,rcw->hcw/dot_general | solution.py:146
  127.0 0.7 copy.219
  127.7 0.7 copy.218
  (88 shorter events, 5.8 us)
Async XLA Ops:
  7.2 8.8 %copy-start.16 = (s32[16]{0:T(128)S(1)}, s32[16]{0:T(128)}, u32[]{:S(2)}) copy-start(s32[16]{0:T(128)} %param.9) | copy-start | bytes 196
  7.2 8.9 %copy-start.15 = (s32[16,3]{0,1:T(4,128)S(1)}, s32[16,3]{0,1:T(4,128)}, u32[]{:S(2)}) copy-start(s32[16,3]{0,1:T(4,128)} %param.10) | copy-start | bytes 580
  7.2 10.2 %copy-start.14 = (bf16[256,1024]{1,0:T(8,128)(2,1)S(1)}, bf16[256,1024]{1,0:T(8,128)(2,1)}, u32[]{:S(2)}) copy-start(bf16[256,1024]{1,0:T(8,128)(2,1)} %param.6) | copy-start | bytes 1572868
  7.2 55.7 %all-gather.2.cloned.1.call-start = ((), (), s32[]{:S(2)}) async-start(), calls=%async_computation.3 | async-start | bytes 2359296 | tf_op jit(solution)/shard_map/all_gather | solution.py:98
  9.1 0.7 copy-start.9
  9.9 7.5 %copy-start.10 = (bf16[256,512]{1,0:T(8,128)(2,1)S(1)}, bf16[256,512]{1,0:T(8,128)(2,1)}, u32[]{:S(2)}) copy-start(bf16[256,512]{1,0:T(8,128)(2,1)} %copy-done.9) | copy-start | bytes 786436
  11.8 13.1 %all-to-all-start.1 = ((bf16[64,4,1024]{2,0,1:T(8,128)(2,1)}), bf16[64,4,1024]{2,0,1:T(8,128)(2,1)S(1)}, u32[]{:S(2)}, u32[]{:S(2)}) async-start(bf16[64,4,1024]{2,0,1:T(8,128)(2,1)} %bitcast.175), calls=%async_computation.1 | async-start | bytes 1048576 | tf_op jit(solution)/shard_map/all_to_all | solution.py:82
  68.8 0.8 copy-start.13
  70.2 1.3 copy-start.4
  71.5 1.0 copy-start
  74.5 1.6 %copy-start.5 = (bf16[2,128,4,128]{3,1,2,0:T(8,128)(2,1)S(1)}, bf16[2,128,4,128]{3,1,2,0:T(8,128)(2,1)}, u32[]{:S(2)}) copy-start(bf16[2,128,4,128]{3,1,2,0:T(8,128)(2,1)} %copy-done.4) | copy-start | bytes 786436
  75.3 0.7 copy-start.6
  81.2 13.0 %all-to-all-start = ((bf16[4,64,1024]{2,1,0:T(8,128)(2,1)}), bf16[4,64,1024]{2,1,0:T(8,128)(2,1)}, u32[]{:S(2)}, u32[]{:S(2)}) async-start(bf16[4,64,1024]{2,1,0:T(8,128)(2,1)} %all_to_all.29), calls=%async_computation | async-start | bytes 1048576 | tf_op jit(solution)/shard_map/all_to_all | solution.py:154
  85.5 2.3 %copy-start.7 = (bf16[2,128,4,128]{3,1,2,0:T(8,128)(2,1)S(1)}, bf16[2,128,4,128]{3,1,2,0:T(8,128)(2,1)}, u32[]{:S(2)}) copy-start(bf16[2,128,4,128]{3,1,2,0:T(8,128)(2,1)} %copy-done.6) | copy-start | bytes 786436
  85.5 2.3 %copy-start.11 = (bf16[128,2,4,128]{0,3,2,1:T(8,128)(2,1)S(1)}, bf16[128,2,4,128]{0,3,2,1:T(8,128)(2,1)}, u32[]{:S(2)}) copy-start(bf16[128,2,4,128]{0,3,2,1:T(8,128)(2,1)} %copy.192) | copy-start | bytes 786436
  85.5 2.4 %copy-start.3 = (bf16[128,2,4,128,1]{0,3,2,4,1:T(8,128)(2,1)S(1)}, bf16[128,2,4,128,1]{0,3,2,4,1:T(8,128)(2,1)}, u32[]{:S(2)}) copy-start(bf16[128,2,4,128,1]{0,3,2,4,1:T(8,128)(2,1)} %copy.244) | copy-start | bytes 786436
  87.9 1.0 copy-start.8
  88.8 1.0 copy-start.2
  92.3 6.6 %copy-start.1 = (bf16[2,4,128,4,128]{2,4,1,3,0:T(8,128)(2,1)S(1)}, bf16[2,4,128,4,128]{2,4,1,3,0:T(8,128)(2,1)}, u32[]{:S(2)}) copy-start(bf16[2,4,128,4,128]{2,4,1,3,0:T(8,128)(2,1)} %copy-done) | copy-start | bytes 3145732
  93.7 6.6 %copy-start.12 = (bf16[4,128,256]{1,2,0:T(8,128)(2,1)S(1)}, bf16[4,128,256]{1,2,0:T(8,128)(2,1)}, u32[]{:S(2)}) copy-start(bf16[4,128,256]{1,2,0:T(8,128)(2,1)} %get-tuple-element.39) | copy-start | bytes 786436
  94.3 30.2 %all-to-all-start.2 = ((bf16[8,128,512]{2,1,0:T(8,128)(2,1)}), bf16[8,128,512]{2,1,0:T(8,128)(2,1)}, u32[]{:S(2)}, u32[]{:S(2)}) async-start(bf16[8,128,512]{2,1,0:T(8,128)(2,1)} %copy.216), calls=%async_computation.2 | async-start | bytes 2097152 | tf_op jit(solution)/shard_map/all_to_all | solution.py:144
Sparse Core Ops, SparseCore 0:
  10.7 52.1 all-gather.1
where the time goes:
time: 136 us; the launch traced here: 135 us
  waiting for transfers between devices  60.4 us (44%)
  local copies, waits for them, and re-layouts  28.4 us (21%)
  between operations  14.6 us (11%)
  matrix products  13.8 us (10%)
  starting transfers between devices  12.8 us (9%)
  other arithmetic  5.13 us (4%)
    all_gather x1, waiting for transfers between devices, body(): shard_part = lax.all_gather(paired, 'seq', axis=0, tiled=True)  35.4 us
    all_to_all x1, waiting for transfers between devices, body(): lax.all_to_all(bundle, 'seq', split_axis=0, concat_axis=0, tiled=True)  18.8 us
    all_to_all x1, waiting for transfers between devices, body(): lax.all_to_all(cotangent, 'head', split_axis=1, concat_axis=0, tiled=True)  5.56 us
    gather x2, local copies, waits for them, and re-layouts, body(): jnp.take(shard_part, jnp.clip(row_index, 0, piece_rows - 1).reshape(-1),...  4.93 us
    all_to_all x1, starting transfers between devices, body(): lax.all_to_all(attended_all, 'head', split_axis=0, concat_axis=1, tiled=T...  4.31 us
    all_to_all x1, starting transfers between devices, body(): lax.all_to_all(bundle, 'seq', split_axis=0, concat_axis=0, tiled=True)  4.24 us
    unnamed x37, local copies, waits for them, and re-layouts  4.23 us
    all_to_all x1, starting transfers between devices, body(): lax.all_to_all(cotangent, 'head', split_axis=1, concat_axis=0, tiled=True)  4.21 us
  transfers between devices with their start and end apart: 4, of which 4 were waited for; matrix products, arithmetic and copies ran while one was open for 17% of the time, Pallas kernels for 0%

commit v1 on v0

v1 whole, which is shorter than its diff:
```python
import functools
import math

import jax
import jax.numpy as jnp
from jax import lax
from jax.experimental import pallas as pl
from jax.experimental.pallas import tpu as pltpu
from jax.sharding import PartitionSpec as P

HEAD_DIM = 128
HIDDEN = -1e30


def dot(left, right, left_dim, right_dim):
    return lax.dot_general(
        left, right, (((left_dim,), (right_dim,)), ((), ())), preferred_element_type=jnp.float32
    )


def kernel(
    dims,
    place_ref,
    lists_ref,
    q_ref,
    k_ref,
    v_ref,
    cot_ref,
    att_ref,
    qg_ref,
    kg_ref,
    vg_ref,
    half_tab,
    owner_tab,
    valid_tab,
    do_buf,
    att_buf,
    kv_send,
    kv_recv,
    g_send,
    g_recv,
    parts,
    own_acc,
    local_sem,
    cot_ssem,
    cot_rsem,
    att_ssem,
    att_rsem,
    kv_ssem,
    kv_rsem,
    g_ssem,
    g_rsem,
):
    n, heads, span, picks, kv_local, group = dims
    me = lax.axis_index("seq")
    hd = lax.axis_index("head")
    rows = 2 * span // heads
    width = kv_local * group * HEAD_DIM
    gwidth = group * HEAD_DIM
    scale = 1.0 / math.sqrt(HEAD_DIM)

    barrier = pltpu.get_barrier_semaphore()

    def greet_seq(step, carry):
        peer = lax.rem(me + step, n)
        pl.semaphore_signal(barrier, inc=1, device_id={"seq": peer})
        return carry

    def greet_head(step, carry):
        peer = lax.rem(hd + step, heads)
        pl.semaphore_signal(barrier, inc=1, device_id={"head": peer})
        return carry

    lax.fori_loop(1, n, greet_seq, 0)
    lax.fori_loop(1, heads, greet_head, 0)

    my_second = place_ref[2 * me + 1]

    def fill_half(peer, carry):
        wants = jnp.int32(0)
        for side in range(2):
            block = place_ref[2 * peer + side]
            for pick in range(picks):
                wants = jnp.where(lists_ref[block, pick] == my_second, 1, wants)
        half_tab[peer] = wants
        return carry

    lax.fori_loop(0, n, fill_half, 0)

    spare = lax.rem(me + 1, n)
    for side in range(2):
        own = place_ref[2 * me + side]
        blocks = [lists_ref[own, pick] for pick in range(picks)]
        for pick in range(picks):
            block = blocks[pick]
            valid = jnp.where(block != own, 1, 0)
            for before in range(pick):
                valid = jnp.where(block == blocks[before], 0, valid)

            def find(at, owner, block=block):
                hit = (place_ref[2 * at] == block) | (place_ref[2 * at + 1] == block)
                return jnp.where(hit, at, owner)

            owner = lax.fori_loop(0, n, find, jnp.int32(0))
            owner_tab[side * picks + pick] = jnp.where(valid == 1, owner, spare)
            valid_tab[side * picks + pick] = valid

    pl.semaphore_wait(barrier, n - 1 + heads - 1)

    def cot_copy(peer, slot):
        return pltpu.make_async_remote_copy(
            src_ref=cot_ref.at[:, pl.ds(pl.multiple_of(peer * width, width), width)],
            dst_ref=do_buf.at[pl.ds(pl.multiple_of(slot * rows, rows), rows), :],
            send_sem=cot_ssem.at[peer],
            recv_sem=cot_rsem.at[slot],
            device_id={"head": peer},
        )

    def att_copy(peer, slot, g):
        return pltpu.make_async_remote_copy(
            src_ref=att_buf.at[
                pl.ds(pl.multiple_of(peer * rows, rows), rows), pl.ds(g * gwidth, gwidth)
            ],
            dst_ref=att_ref.at[
                :, pl.ds(pl.multiple_of(slot * width + g * gwidth, gwidth), gwidth)
            ],
            send_sem=att_ssem.at[g, peer],
            recv_sem=att_rsem.at[g, slot],
            device_id={"head": peer},
        )

    def kv_copy(peer, slot, g):
        return pltpu.make_async_remote_copy(
            src_ref=kv_send.at[g, peer],
            dst_ref=kv_recv[g].at[slot],
            send_sem=kv_ssem.at[g, peer],
            recv_sem=kv_rsem.at[g, slot],
            device_id={"seq": peer},
        )

    def grad_copy(peer, slot, g):
        return pltpu.make_async_remote_copy(
            src_ref=g_send.at[g, peer],
            dst_ref=g_recv.at[g, slot],
            send_sem=g_ssem.at[g, peer],
            recv_sem=g_rsem.at[g, slot],
            device_id={"seq": peer},
        )

    def over_seq(action):
        def one(step, carry):
            action(lax.rem(me + step, n))
            return carry

        lax.fori_loop(1, n, one, 0)

    def over_head(action):
        def one(step, carry):
            action(lax.rem(hd + step, heads))
            return carry

        lax.fori_loop(1, heads, one, 0)

    over_head(lambda peer: cot_copy(peer, hd).start())

    for g in range(kv_local):
        cols = slice(g * HEAD_DIM, (g + 1) * HEAD_DIM)

        def send_kv(peer, g=g, cols=cols):
            second = half_tab[peer] == 1
            kv_send[g, peer, :, :HEAD_DIM] = jnp.where(second, k_ref[span:, cols], k_ref[:span, cols])
            kv_send[g, peer, :, HEAD_DIM:] = jnp.where(second, v_ref[span:, cols], v_ref[:span, cols])
            kv_copy(peer, me, g).start()

        over_seq(send_kv)

    own_cot = pltpu.make_async_copy(
        cot_ref.at[:, pl.ds(pl.multiple_of(hd * width, width), width)],
        do_buf.at[pl.ds(pl.multiple_of(hd * rows, rows), rows), :],
        local_sem.at[0],
    )
    own_cot.start()
    own_cot.wait()
    over_head(lambda peer: cot_copy(hd, peer).wait_recv())

    pair = 2
    lanes = pair * span
    key_at = lax.broadcasted_iota(jnp.int32, (span, lanes), 0)
    query_at = lax.rem(lax.broadcasted_iota(jnp.int32, (span, lanes), 1), span)
    causal = key_at <= query_at

    for g in range(kv_local):
        cols = slice(g * HEAD_DIM, (g + 1) * HEAD_DIM)
        over_seq(lambda peer, g=g: kv_copy(me, peer, g).wait_recv())

        def attend(side, carry, g=g, cols=cols):
            base = pl.multiple_of(side * span, span)
            here = pl.ds(base, span)
            keys = [k_ref[here, cols]]
            values = [v_ref[here, cols]]
            valid = []
            for pick in range(picks):
                owner = owner_tab[side * picks + pick]
                keys.append(kv_recv[g][owner, :, :HEAD_DIM])
                values.append(kv_recv[g][owner, :, HEAD_DIM:])
                valid.append(valid_tab[side * picks + pick] == 1)
            keys = jnp.concatenate(keys, axis=0)
            values = jnp.concatenate(values, axis=0)
            key_sum = None
            for chunk in range(group // pair):
                first = g * group + chunk * pair
                spots = [
                    slice((first + at) * HEAD_DIM, (first + at + 1) * HEAD_DIM)
                    for at in range(pair)
                ]
                query = jnp.concatenate([q_ref[here, spot] for spot in spots], axis=0)
                grad = jnp.concatenate([do_buf[here, spot] for spot in spots], axis=0)
                scores = dot(keys, query, 1, 1) * scale
                masked = [jnp.where(causal, scores[:span], HIDDEN)]
                for pick in range(picks):
                    piece = scores[(pick + 1) * span : (pick + 2) * span]
                    masked.append(jnp.where(valid[pick], piece, HIDDEN))
                scores = jnp.concatenate(masked, axis=0)
                top = jnp.max(scores, axis=0, keepdims=True)
                probs = jnp.exp(scores - top)
                total = jnp.sum(probs, axis=0, keepdims=True)
                probs = probs * (1.0 / total)
                weights = probs.astype(jnp.bfloat16)
                attended = dot(values, weights, 0, 0)
                slopes = dot(values, grad, 1, 1)
                delta = jnp.sum(probs * slopes, axis=0, keepdims=True)
                dscores = (probs * ((slopes - delta) * scale)).astype(jnp.bfloat16)
                query_grad = dot(keys, dscores, 0, 0)
                attended = attended.T.astype(jnp.bfloat16)
                query_grad = query_grad.T.astype(jnp.bfloat16)
                for at in range(pair):
                    att_buf[here, spots[at]] = attended[at * span : (at + 1) * span]
                    qg_ref[here, spots[at]] = query_grad[at * span : (at + 1) * span]
                key_part = dot(dscores, query, 1, 0)
                value_part = dot(weights, grad, 1, 0)
                if key_sum is None:
                    key_sum, value_sum = key_part, value_part
                else:
                    key_sum, value_sum = key_sum + key_part, value_sum + value_part
            own_acc[g, side, :, :HEAD_DIM] = key_sum[:span]
            own_acc[g, side, :, HEAD_DIM:] = value_sum[:span]
            for pick in range(picks):
                piece = slice((pick + 1) * span, (pick + 2) * span)
                parts[g, side * picks + pick, :, :HEAD_DIM] = key_sum[piece].astype(jnp.bfloat16)
                parts[g, side * picks + pick, :, HEAD_DIM:] = value_sum[piece].astype(jnp.bfloat16)
            return carry

        lax.fori_loop(0, 2, attend, 0)

        def send_grad(peer, g=g):
            spot = jnp.int32(0)
            found = jnp.int32(0)
            for at in range(2 * picks):
                hit = (owner_tab[at] == peer) & (valid_tab[at] == 1)
                spot = jnp.where(hit, at, spot)
                found = jnp.where(hit, 1, found)
            part = parts[g, spot]
            g_send[g, peer] = jnp.where(found == 1, part, jnp.zeros_like(part))
            grad_copy(peer, me, g).start()

        over_seq(send_grad)
        over_head(lambda peer, g=g: att_copy(peer, hd, g).start())

    att_ref[:, pl.ds(pl.multiple_of(hd * width, width), width)] = att_buf[
        pl.ds(pl.multiple_of(hd * rows, rows), rows), :
    ]

    for g in range(kv_local):
        cols = slice(g * HEAD_DIM, (g + 1) * HEAD_DIM)

        def add_grad(peer, g=g):
            grad_copy(me, peer, g).wait_recv()
            part = g_recv[g, peer].astype(jnp.float32)
            second = half_tab[peer] == 1
            own_acc[g, 0] += jnp.where(second, 0.0, part)
            own_acc[g, 1] += jnp.where(second, part, 0.0)

        over_seq(add_grad)
        for side in range(2):
            here = slice(side * span, (side + 1) * span)
            kg_ref[here, cols] = own_acc[g, side, :, :HEAD_DIM].astype(jnp.bfloat16)
            vg_ref[here, cols] = own_acc[g, side, :, HEAD_DIM:].astype(jnp.bfloat16)

    over_head(lambda peer: cot_copy(peer, hd).wait_send())
    for g in range(kv_local):
        over_head(lambda peer, g=g: att_copy(hd, peer, g).wait_recv())
        over_head(lambda peer, g=g: att_copy(peer, hd, g).wait_send())
        over_seq(lambda peer, g=g: kv_copy(peer, me, g).wait_send())
        over_seq(lambda peer, g=g: grad_copy(peer, me, g).wait_send())


def body(queries, key_rows, value_rows, span_place, block_lists, cotangent):
    n = lax.axis_size("seq")
    heads = lax.axis_size("head")
    span = queries.shape[0] // 2
    picks = block_lists.shape[1]
    kv_local = key_rows.shape[1] // HEAD_DIM
    group = queries.shape[1] // key_rows.shape[1]
    bf16 = jnp.bfloat16
    vmem = pl.BlockSpec(memory_space=pltpu.VMEM)
    smem = pl.BlockSpec(memory_space=pltpu.SMEM)
    box = (kv_local, n, span, 2 * HEAD_DIM)
    dma = pltpu.SemaphoreType.DMA
    flops = 6 * 2 * 2 * span * span * (picks + 1) * queries.shape[1]
    return pl.pallas_call(
        functools.partial(kernel, (n, heads, span, picks, kv_local, group)),
        out_shape=[
            jax.ShapeDtypeStruct(cotangent.shape, bf16),
            jax.ShapeDtypeStruct(queries.shape, bf16),
            jax.ShapeDtypeStruct(key_rows.shape, bf16),
            jax.ShapeDtypeStruct(value_rows.shape, bf16),
        ],
        in_specs=[smem, smem, vmem, vmem, vmem, vmem],
        out_specs=[vmem] * 4,
        scratch_shapes=[
            pltpu.SMEM((n,), jnp.int32),
            pltpu.SMEM((2 * picks,), jnp.int32),
            pltpu.SMEM((2 * picks,), jnp.int32),
            pltpu.VMEM(queries.shape, bf16),
            pltpu.VMEM(queries.shape, bf16),
            pltpu.VMEM(box, bf16),
            [pltpu.VMEM(box[1:], bf16)] * kv_local,
            pltpu.VMEM(box, bf16),
            pltpu.VMEM(box, bf16),
            pltpu.VMEM((kv_local, 2 * picks, span, 2 * HEAD_DIM), bf16),
            pltpu.VMEM((kv_local, 2, span, 2 * HEAD_DIM), jnp.float32),
            dma((1,)),
            dma((heads,)),
            dma((heads,)),
            dma((kv_local, heads)),
            dma((kv_local, heads)),
            dma((kv_local, n)),
            dma((kv_local, n)),
            dma((kv_local, n)),
            dma((kv_local, n)),
        ],
        compiler_params=pltpu.CompilerParams(
            collective_id=0, has_side_effects=True, vmem_limit_bytes=48 * 1024 * 1024
        ),
        cost_estimate=pl.CostEstimate(
            flops=flops, bytes_accessed=4 * queries.size * 2, transcendentals=flops // 1536
        ),
    )(span_place, block_lists, queries, key_rows, value_rows, cotangent)


def solution(mesh):
    in_specs = (
        P("seq", "head"),
        P("seq", "head"),
        P("seq", "head"),
        P(),
        P(),
        P(("seq", "head"), None),
    )
    out_specs = (P(("seq", "head"), None), P("seq", "head"), P("seq", "head"), P("seq", "head"))
    return jax.shard_map(body, mesh=mesh, in_specs=in_specs, out_specs=out_specs, check_vma=False)
```

time: 136 us -> 60.4 us (0.44)
  waiting for transfers between devices: 60.4 us -> 0 us
  Pallas kernels: 0 us -> 51.2 us
  local copies, waits for them, and re-layouts: 28.4 us -> 7.56 us
  between operations: 14.6 us -> 0.65 us
  matrix products: 13.8 us -> 0 us
  starting transfers between devices: 12.8 us -> 0 us
  other arithmetic: 5.13 us -> 0 us
    pallas_call x0 -> x1, Pallas kernels: none -> 51.2 us  [body(): pl.pallas_call(functools.partial(kernel, (n, heads, span, picks, kv_local...]
    all_gather x1 -> x0, waiting for transfers between devices: 35.4 us -> none  [body(): shard_part = lax.all_gather(paired, 'seq', axis=0, tiled=True)]
    all_to_all x3 -> x0, waiting for transfers between devices: 25 us -> none  [the longest x1 18.8 us: body(): lax.all_to_all(bundle, 'seq', split_axis=0, concat_axis=0, tiled=True)]
    dot_general x14 -> x0, matrix products: 13.8 us -> none  [the longest x2 2.81 us: attend_block(): jnp.einsum('kgcje,ckgd->jekd', weights, grad_block, preferred_element_typ...]
    all_to_all x3 -> x0, starting transfers between devices: 12.8 us -> none  [the longest x1 4.31 us: body(): lax.all_to_all(attended_all, 'head', split_axis=0, concat_axis=1, tiled=T...]
    all_to_all x3 -> x0, local copies, waits for them, and re-layouts: 5.99 us -> none  [the longest x2 4.07 us: body(): lax.all_to_all(attended_all, 'head', split_axis=0, concat_axis=1, tiled=T...]
    gather x2 -> x0, local copies, waits for them, and re-layouts: 4.93 us -> none  [body(): jnp.take(shard_part, jnp.clip(row_index, 0, piece_rows - 1).reshape(-1),...]
    unnamed x37 -> x15, local copies, waits for them, and re-layouts: 4.23 us -> 7.56 us
  transfers between devices with their start and end apart: 4 -> 0, of which waited for: 4 -> 0; matrix products, arithmetic and copies ran while one was open for 17% -> 0% of each run, Pallas kernels for 0% -> 0%
where the time goes in v1:
time: 60.4 us; the launch traced here: 59.4 us
  Pallas kernels  51.2 us (85%)
  local copies, waits for them, and re-layouts  7.56 us (13%)
  between operations  0.65 us (1%)
    pallas_call x1, Pallas kernels, body(): pl.pallas_call(functools.partial(kernel, (n, heads, span, picks, kv_local...  51.2 us
    unnamed x15, local copies, waits for them, and re-layouts  7.56 us

profile of v1, /device:TPU:0, one launch (start us, length us, event | category | flops | bytes accessed | tf_op | source)
XLA Modules:
  0.0 59.4 jit_solution(13828959320784513357)
XLA Ops:
  0.6 0.0 copy-start.4
  0.6 0.8 %copy.10.lists_ref = s32[16,3]{1,0:T(8,128)S(1)} copy(s32[16,3]{0,1:T(4,128)} %param.10) | data formatting | bytes 384 | tf_op args[4]
  1.4 0.0 copy-done.4
  1.4 0.0 copy-start
  1.4 1.0 %copy-done = bf16[256,1024]{1,0:T(8,128)(2,1)S(1)} copy-done((bf16[256,1024]{1,0:T(8,128)(2,1)S(1)}, bf16[256,1024]{1,0:T(8,128)(2,1)}, u32[]{:S(2)}) %copy-start) | copy-done | bytes 524312
  2.5 0.0 copy-start.1
  2.5 1.0 %copy-done.1 = bf16[64,4096]{1,0:T(8,128)(2,1)S(1)} copy-done((bf16[64,4096]{1,0:T(8,128)(2,1)S(1)}, bf16[64,4096]{1,0:T(8,128)(2,1)}, u32[]{:S(2)}) %copy-start.1) | copy-done | bytes 524312
  3.5 0.0 copy-start.2
  3.5 0.9 %copy-done.2 = bf16[256,256]{1,0:T(8,128)(2,1)S(1)} copy-done((bf16[256,256]{1,0:T(8,128)(2,1)S(1)}, bf16[256,256]{1,0:T(8,128)(2,1)}, u32[]{:S(2)}) %copy-start.2) | copy-done | bytes 131096
  4.4 0.0 copy-start.3
  4.4 0.9 %copy-done.3 = bf16[256,256]{1,0:T(8,128)(2,1)S(1)} copy-done((bf16[256,256]{1,0:T(8,128)(2,1)S(1)}, bf16[256,256]{1,0:T(8,128)(2,1)}, u32[]{:S(2)}) %copy-start.3) | copy-done | bytes 131096
  5.3 51.2 %shard_map.93 = (bf16[64,4096]{1,0:T(8,128)(2,1)S(1)}, bf16[256,1024]{1,0:T(8,128)(2,1)S(1)}, bf16[256,256]{1,0:T(8,128)(2,1)S(1)}, bf16[256,256]{1,0:T(8,128)(2,1)S(1)}) custom-call(s32[16]{0:T(128)S(1)} %copy-done.4, s32[16,3]{1,0:T(8,128)S(1)} %copy.10.lists_ref, bf16[256,1024]{1,0:T(8,128)(2,1)S(1)} %copy-done, bf16[256,256]{1,0:T(8,128)(2,1)S(1)} %copy-done.2, ...), custom_call_target="tpu_custom_call" | custom-call | flops 1610612736 | bytes 2097152 | tf_op jit(solution)/shard_map/pallas_call | solution.py:310
  56.5 0.8 %copy.15 = bf16[64,4096]{1,0:T(8,128)(2,1)} copy(bf16[64,4096]{1,0:T(8,128)(2,1)S(1)} %get-tuple-element.8) | data formatting | bytes 1048576
  57.3 0.8 %copy.16 = bf16[256,1024]{1,0:T(8,128)(2,1)} copy(bf16[256,1024]{1,0:T(8,128)(2,1)S(1)} %get-tuple-element.9) | data formatting | bytes 1048576
  58.1 0.7 %copy.17 = bf16[256,256]{1,0:T(8,128)(2,1)} copy(bf16[256,256]{1,0:T(8,128)(2,1)S(1)} %get-tuple-element.10) | data formatting | bytes 262144
  58.7 0.7 %copy.18 = bf16[256,256]{1,0:T(8,128)(2,1)} copy(bf16[256,256]{1,0:T(8,128)(2,1)S(1)} %get-tuple-element.11) | data formatting | bytes 262144
Async XLA Ops:
  0.6 0.8 %copy-start.4 = (s32[16]{0:T(128)S(1)}, s32[16]{0:T(128)}, u32[]{:S(2)}) copy-start(s32[16]{0:T(128)} %place_ref.1) | copy-start | bytes 196
  1.4 1.0 %copy-start = (bf16[256,1024]{1,0:T(8,128)(2,1)S(1)}, bf16[256,1024]{1,0:T(8,128)(2,1)}, u32[]{:S(2)}) copy-start(bf16[256,1024]{1,0:T(8,128)(2,1)} %q_ref.1) | copy-start | bytes 1572868
  2.5 1.0 %copy-start.1 = (bf16[64,4096]{1,0:T(8,128)(2,1)S(1)}, bf16[64,4096]{1,0:T(8,128)(2,1)}, u32[]{:S(2)}) copy-start(bf16[64,4096]{1,0:T(8,128)(2,1)} %cot_ref.1) | copy-start | bytes 1572868
  3.5 0.9 %copy-start.2 = (bf16[256,256]{1,0:T(8,128)(2,1)S(1)}, bf16[256,256]{1,0:T(8,128)(2,1)}, u32[]{:S(2)}) copy-start(bf16[256,256]{1,0:T(8,128)(2,1)} %k_ref.1) | copy-start | bytes 393220
  4.4 0.9 %copy-start.3 = (bf16[256,256]{1,0:T(8,128)(2,1)S(1)}, bf16[256,256]{1,0:T(8,128)(2,1)}, u32[]{:S(2)}) copy-start(bf16[256,256]{1,0:T(8,128)(2,1)} %v_ref.1) | copy-start | bytes 393220

commit v2 on v1

--- a/solution.py
+++ b/solution.py
@@ -10,6 +10,7 @@
 
 HEAD_DIM = 128
 HIDDEN = -1e30
+VMEM_BYTES = 64 * 1024 * 1024
 
 
 def dot(left, right, left_dim, right_dim):
@@ -22,17 +23,23 @@
     dims,
     place_ref,
     lists_ref,
+    q_in,
+    k_in,
+    v_in,
+    cot_ref,
+    att_ref,
+    qg_out,
+    kg_out,
+    vg_out,
+    half_tab,
+    owner_tab,
+    valid_tab,
     q_ref,
     k_ref,
     v_ref,
-    cot_ref,
-    att_ref,
     qg_ref,
     kg_ref,
     vg_ref,
-    half_tab,
-    owner_tab,
-    valid_tab,
     do_buf,
     att_buf,
     kv_send,
@@ -59,6 +66,20 @@
     gwidth = group * HEAD_DIM
     scale = 1.0 / math.sqrt(HEAD_DIM)
 
+    fetches = [
+        pltpu.make_async_copy(source, target, local_sem.at[at])
+        for at, (source, target) in enumerate(((k_in, k_ref), (v_in, v_ref), (q_in, q_ref)))
+    ]
+    fetches.append(
+        pltpu.make_async_copy(
+            cot_ref.at[:, pl.ds(pl.multiple_of(hd * width, width), width)],
+            do_buf.at[pl.ds(pl.multiple_of(hd * rows, rows), rows), :],
+            local_sem.at[3],
+        )
+    )
+    for fetch in fetches:
+        fetch.start()
+
     barrier = pltpu.get_barrier_semaphore()
 
     def greet_seq(step, carry):
@@ -81,7 +102,7 @@
         for side in range(2):
             block = place_ref[2 * peer + side]
             for pick in range(picks):
-                wants = jnp.where(lists_ref[block, pick] == my_second, 1, wants)
+                wants = jnp.where(lists_ref[pick, block] == my_second, 1, wants)
         half_tab[peer] = wants
         return carry
 
@@ -90,7 +111,7 @@
     spare = lax.rem(me + 1, n)
     for side in range(2):
         own = place_ref[2 * me + side]
-        blocks = [lists_ref[own, pick] for pick in range(picks)]
+        blocks = [lists_ref[pick, own] for pick in range(picks)]
         for pick in range(picks):
             block = blocks[pick]
             valid = jnp.where(block != own, 1, 0)
@@ -162,6 +183,8 @@
         lax.fori_loop(1, heads, one, 0)
 
     over_head(lambda peer: cot_copy(peer, hd).start())
+    fetches[0].wait()
+    fetches[1].wait()
 
     for g in range(kv_local):
         cols = slice(g * HEAD_DIM, (g + 1) * HEAD_DIM)
@@ -174,13 +197,8 @@
 
         over_seq(send_kv)
 
-    own_cot = pltpu.make_async_copy(
-        cot_ref.at[:, pl.ds(pl.multiple_of(hd * width, width), width)],
-        do_buf.at[pl.ds(pl.multiple_of(hd * rows, rows), rows), :],
-        local_sem.at[0],
-    )
-    own_cot.start()
-    own_cot.wait()
+    fetches[2].wait()
+    fetches[3].wait()
     over_head(lambda peer: cot_copy(hd, peer).wait_recv())
 
     pair = 2
@@ -266,9 +284,22 @@
         over_seq(send_grad)
         over_head(lambda peer, g=g: att_copy(peer, hd, g).start())
 
-    att_ref[:, pl.ds(pl.multiple_of(hd * width, width), width)] = att_buf[
-        pl.ds(pl.multiple_of(hd * rows, rows), rows), :
+    leaving = [
+        pltpu.make_async_copy(source, target, local_sem.at[at])
+        for at, (source, target) in enumerate(
+            (
+                (
+                    att_buf.at[pl.ds(pl.multiple_of(hd * rows, rows), rows), :],
+                    att_ref.at[:, pl.ds(pl.multiple_of(hd * width, width), width)],
+                ),
+                (qg_ref, qg_out),
+                (kg_ref, kg_out),
+                (vg_ref, vg_out),
+            )
+        )
     ]
+    leaving[0].start()
+    leaving[1].start()
 
     for g in range(kv_local):
         cols = slice(g * HEAD_DIM, (g + 1) * HEAD_DIM)
@@ -286,12 +317,28 @@
             kg_ref[here, cols] = own_acc[g, side, :, :HEAD_DIM].astype(jnp.bfloat16)
             vg_ref[here, cols] = own_acc[g, side, :, HEAD_DIM:].astype(jnp.bfloat16)
 
+    leaving[2].start()
+    leaving[3].start()
     over_head(lambda peer: cot_copy(peer, hd).wait_send())
     for g in range(kv_local):
         over_head(lambda peer, g=g: att_copy(hd, peer, g).wait_recv())
         over_head(lambda peer, g=g: att_copy(peer, hd, g).wait_send())
         over_seq(lambda peer, g=g: kv_copy(peer, me, g).wait_send())
         over_seq(lambda peer, g=g: grad_copy(peer, me, g).wait_send())
+    for copy in leaving:
+        copy.wait()
+
+
+def write_out(*refs):
+    sources, targets, sems = refs[:4], refs[4:8], refs[8]
+    copies = [
+        pltpu.make_async_copy(source, target, sems.at[at])
+        for at, (source, target) in enumerate(zip(sources, targets))
+    ]
+    for copy in copies:
+        copy.start()
+    for copy in copies:
+        copy.wait()
 
 
 def body(queries, key_rows, value_rows, span_place, block_lists, cotangent):
@@ -302,12 +349,12 @@
     kv_local = key_rows.shape[1] // HEAD_DIM
     group = queries.shape[1] // key_rows.shape[1]
     bf16 = jnp.bfloat16
-    vmem = pl.BlockSpec(memory_space=pltpu.VMEM)
+    hbm = pl.BlockSpec(memory_space=pltpu.HBM)
     smem = pl.BlockSpec(memory_space=pltpu.SMEM)
     box = (kv_local, n, span, 2 * HEAD_DIM)
     dma = pltpu.SemaphoreType.DMA
     flops = 6 * 2 * 2 * span * span * (picks + 1) * queries.shape[1]
-    return pl.pallas_call(
+    results = pl.pallas_call(
         functools.partial(kernel, (n, heads, span, picks, kv_local, group)),
         out_shape=[
             jax.ShapeDtypeStruct(cotangent.shape, bf16),
@@ -315,12 +362,18 @@
             jax.ShapeDtypeStruct(key_rows.shape, bf16),
             jax.ShapeDtypeStruct(value_rows.shape, bf16),
         ],
-        in_specs=[smem, smem, vmem, vmem, vmem, vmem],
-        out_specs=[vmem] * 4,
+        in_specs=[smem, smem, hbm, hbm, hbm, hbm],
+        out_specs=[hbm] * 4,
         scratch_shapes=[
             pltpu.SMEM((n,), jnp.int32),
             pltpu.SMEM((2 * picks,), jnp.int32),
             pltpu.SMEM((2 * picks,), jnp.int32),
+            pltpu.VMEM(queries.shape, bf16),
+            pltpu.VMEM(key_rows.shape, bf16),
+            pltpu.VMEM(value_rows.shape, bf16),
+            pltpu.VMEM(queries.shape, bf16),
+            pltpu.VMEM(key_rows.shape, bf16),
+            pltpu.VMEM(value_rows.shape, bf16),
             pltpu.VMEM(queries.shape, bf16),
             pltpu.VMEM(queries.shape, bf16),
             pltpu.VMEM(box, bf16),
@@ -329,7 +382,7 @@
             pltpu.VMEM(box, bf16),
             pltpu.VMEM((kv_local, 2 * picks, span, 2 * HEAD_DIM), bf16),
             pltpu.VMEM((kv_local, 2, span, 2 * HEAD_DIM), jnp.float32),
-            dma((1,)),
+            dma((4,)),
             dma((heads,)),
             dma((heads,)),
             dma((kv_local, heads)),
@@ -340,12 +393,22 @@
             dma((kv_local, n)),
         ],
         compiler_params=pltpu.CompilerParams(
-            collective_id=0, has_side_effects=True, vmem_limit_bytes=48 * 1024 * 1024
+            collective_id=0, has_side_effects=True, vmem_limit_bytes=VMEM_BYTES
         ),
         cost_estimate=pl.CostEstimate(
             flops=flops, bytes_accessed=4 * queries.size * 2, transcendentals=flops // 1536
         ),
-    )(span_place, block_lists, queries, key_rows, value_rows, cotangent)
+    )(span_place, block_lists.T, queries, key_rows, value_rows, cotangent)
+    return tuple(
+        pl.pallas_call(
+            write_out,
+            out_shape=[jax.ShapeDtypeStruct(item.shape, item.dtype) for item in results],
+            in_specs=[hbm] * 4,
+            out_specs=[hbm] * 4,
+            scratch_shapes=[dma((4,))],
+            compiler_params=pltpu.CompilerParams(vmem_limit_bytes=VMEM_BYTES),
+        )(*results)
+    )
 
 
 def solution(mesh):

time: 60.4 us -> 94 us (1.56)
  Pallas kernels: 51.2 us -> 92.4 us
  local copies, waits for them, and re-layouts: 7.56 us -> 0 us
    pallas_call x0 -> x1, Pallas kernels: none -> 40.8 us  [body(): pl.pallas_call(write_out, out_shape=[jax.ShapeDtypeStruct(item.shape, ite...]
    unnamed x15 -> x0, local copies, waits for them, and re-layouts: 7.56 us -> none
where the time goes in v2:
time: 94 us; the launch traced here: 93 us
  Pallas kernels  92.4 us (98%)
    pallas_call x1, Pallas kernels, body(): pl.pallas_call(functools.partial(kernel, (n, heads, span, picks, kv_local...  51.5 us
    pallas_call x1, Pallas kernels, body(): pl.pallas_call(write_out, out_shape=[jax.ShapeDtypeStruct(item.shape, ite...  40.8 us

profile of v2, /device:TPU:0, one launch (start us, length us, event | category | flops | bytes accessed | tf_op | source)
XLA Modules:
  0.0 93.0 jit_solution(1487728262835246297)
XLA Ops:
  0.6 51.5 %shard_map.93 = (bf16[64,4096]{1,0:T(8,128)(2,1)}, bf16[256,1024]{1,0:T(8,128)(2,1)}, bf16[256,256]{1,0:T(8,128)(2,1)}, bf16[256,256]{1,0:T(8,128)(2,1)}) custom-call(s32[16]{0:T(128)} %place_ref.1, s32[3,16]{1,0:T(4,128)} %bitcast.1, bf16[256,1024]{1,0:T(8,128)(2,1)} %q_in.1, bf16[256,256]{1,0:T(8,128)(2,1)} %k_in.1, bf16[256,256]{1,0:T(8,128)(2,1)} %v_in.1, ...), custom_call_target="tpu_custom_call" | custom-call | flops 1610612736 | bytes 2097152 | tf_op jit(solution)/shard_map/pallas_call | solution.py:357
  52.2 40.8 %shard_map.94 = (bf16[64,4096]{1,0:T(8,128)(2,1)}, bf16[256,1024]{1,0:T(8,128)(2,1)}, bf16[256,256]{1,0:T(8,128)(2,1)}, bf16[256,256]{1,0:T(8,128)(2,1)}) custom-call(bf16[64,4096]{1,0:T(8,128)(2,1)} %get-tuple-element.8.refs_0_, bf16[256,1024]{1,0:T(8,128)(2,1)} %get-tuple-element.9.refs_1_, bf16[256,256]{1,0:T(8,128)(2,1)} %get-tuple-element.10.refs_2_, ...), custom_call_target="tpu_custom_call" | custom-call | tf_op jit(solution)/shard_map/pallas_call | solution.py:403

commit v3 on v2

--- a/solution.py
+++ b/solution.py
@@ -330,14 +330,21 @@
 
 
 def write_out(*refs):
-    sources, targets, sems = refs[:4], refs[4:8], refs[8]
-    copies = [
-        pltpu.make_async_copy(source, target, sems.at[at])
-        for at, (source, target) in enumerate(zip(sources, targets))
+    sources, targets, stages, sems = refs[:4], refs[4:8], refs[8:12], refs[12]
+    arrive = [
+        pltpu.make_async_copy(source, stage, sems.at[0, at])
+        for at, (source, stage) in enumerate(zip(sources, stages))
     ]
-    for copy in copies:
+    leave = [
+        pltpu.make_async_copy(stage, target, sems.at[1, at])
+        for at, (stage, target) in enumerate(zip(stages, targets))
+    ]
+    for copy in arrive:
         copy.start()
-    for copy in copies:
+    for at in range(4):
+        arrive[at].wait()
+        leave[at].start()
+    for copy in leave:
         copy.wait()
 
 
@@ -405,7 +412,8 @@
             out_shape=[jax.ShapeDtypeStruct(item.shape, item.dtype) for item in results],
             in_specs=[hbm] * 4,
             out_specs=[hbm] * 4,
-            scratch_shapes=[dma((4,))],
+            scratch_shapes=[pltpu.VMEM(item.shape, item.dtype) for item in results]
+            + [dma((2, 4))],
             compiler_params=pltpu.CompilerParams(vmem_limit_bytes=VMEM_BYTES),
         )(*results)
     )

time: 94 us -> 55.3 us (0.59)
  Pallas kernels: 92.4 us -> 53.7 us
    pallas_call x1, Pallas kernels: 40.8 us -> 2.16 us  [body(): pl.pallas_call(write_out, out_shape=[jax.ShapeDtypeStruct(item.shape, ite...]
where the time goes in v3:
time: 55.3 us; the launch traced here: 54.3 us
  Pallas kernels  53.7 us (97%)
  between operations  0.64 us (1%)
    pallas_call x1, Pallas kernels, body(): pl.pallas_call(functools.partial(kernel, (n, heads, span, picks, kv_local...  51.5 us
    pallas_call x1, Pallas kernels, body(): pl.pallas_call(write_out, out_shape=[jax.ShapeDtypeStruct(item.shape, ite...  2.16 us

profile of v3, /device:TPU:0, one launch (start us, length us, event | category | flops | bytes accessed | tf_op | source)
XLA Modules:
  0.0 54.3 jit_solution(12461683265091733219)
XLA Ops:
  0.6 51.5 %shard_map.93 = (bf16[64,4096]{1,0:T(8,128)(2,1)}, bf16[256,1024]{1,0:T(8,128)(2,1)}, bf16[256,256]{1,0:T(8,128)(2,1)}, bf16[256,256]{1,0:T(8,128)(2,1)}) custom-call(s32[16]{0:T(128)} %place_ref.1, s32[3,16]{1,0:T(4,128)} %bitcast.1, bf16[256,1024]{1,0:T(8,128)(2,1)} %q_in.1, bf16[256,256]{1,0:T(8,128)(2,1)} %k_in.1, bf16[256,256]{1,0:T(8,128)(2,1)} %v_in.1, ...), custom_call_target="tpu_custom_call" | custom-call | flops 1610612736 | bytes 2097152 | tf_op jit(solution)/shard_map/pallas_call | solution.py:364
  52.2 2.2 %shard_map.94 = (bf16[64,4096]{1,0:T(8,128)(2,1)}, bf16[256,1024]{1,0:T(8,128)(2,1)}, bf16[256,256]{1,0:T(8,128)(2,1)}, bf16[256,256]{1,0:T(8,128)(2,1)}) custom-call(bf16[64,4096]{1,0:T(8,128)(2,1)} %get-tuple-element.8.refs_0_, bf16[256,1024]{1,0:T(8,128)(2,1)} %get-tuple-element.9.refs_1_, bf16[256,256]{1,0:T(8,128)(2,1)} %get-tuple-element.10.refs_2_, ...), custom_call_target="tpu_custom_call" | custom-call | tf_op jit(solution)/shard_map/pallas_call | solution.py:410

commit v4 on v3

--- a/solution.py
+++ b/solution.py
@@ -57,6 +57,17 @@
     kv_rsem,
     g_ssem,
     g_rsem,
+    sel_tab,
+    full_send,
+    full_recv,
+    fwd_send,
+    col_recv,
+    comb_send,
+    comb_recv,
+    full_sem,
+    fwd_sem,
+    col_rsem,
+    comb_sem,
 ):
     n, heads, span, picks, kv_local, group = dims
     me = lax.axis_index("seq")
@@ -65,6 +76,28 @@
     width = kv_local * group * HEAD_DIM
     gwidth = group * HEAD_DIM
     scale = 1.0 / math.sqrt(HEAD_DIM)
+
+    relay = n == 8
+    z, y = me // 2, lax.rem(me, 2)
+    is_end = (z == 0) | (z == 3)
+    is_inner = jnp.logical_not(is_end)
+    via = jnp.where(z == 0, 4, 2) + y
+    served = jnp.where(z == 2, 0, 6) + y
+    far_end = jnp.where(z == 2, 6, 0)
+    helped = (2 * z + 1 - y, far_end + y, far_end + 1 - y)
+
+    def far(peer):
+        apart = peer // 2 - z
+        return (apart >= 2) | (apart <= -2)
+
+    def peer_is_end(peer):
+        return (peer // 2 == 0) | (peer // 2 == 3)
+
+    def only(condition, action):
+        if relay:
+            pl.when(condition)(action)
+        else:
+            action()
 
     fetches = [
         pltpu.make_async_copy(source, target, local_sem.at[at])
@@ -108,6 +141,16 @@
 
     lax.fori_loop(0, n, fill_half, 0)
 
+    if relay:
+        end_second = place_ref[2 * served + 1]
+        for at, who in enumerate(helped + (me,)):
+            wants = jnp.int32(0)
+            for side in range(2):
+                block = place_ref[2 * who + side]
+                for pick in range(picks):
+                    wants = jnp.where(lists_ref[pick, block] == end_second, 1, wants)
+            sel_tab[at] = wants
+
     spare = lax.rem(me + 1, n)
     for side in range(2):
         own = place_ref[2 * me + side]
@@ -168,6 +211,43 @@
             device_id={"seq": peer},
         )
 
+    def full_copy(g):
+        return pltpu.make_async_remote_copy(
+            src_ref=full_send.at[g],
+            dst_ref=full_recv.at[g],
+            send_sem=full_sem.at[0, g],
+            recv_sem=full_sem.at[1, g],
+            device_id={"seq": via},
+        )
+
+    def forward_copy(g, at):
+        return pltpu.make_async_remote_copy(
+            src_ref=fwd_send.at[g, at],
+            dst_ref=kv_recv[g].at[served],
+            send_sem=fwd_sem.at[g, at],
+            recv_sem=kv_rsem.at[g, served],
+            device_id={"seq": helped[at]},
+        )
+
+    def collect_copy(peer, slot, g):
+        through = jnp.where(peer // 2 == 0, 4, 2) + lax.rem(peer, 2)
+        return pltpu.make_async_remote_copy(
+            src_ref=g_send.at[g, peer],
+            dst_ref=col_recv.at[g, slot],
+            send_sem=g_ssem.at[g, peer],
+            recv_sem=col_rsem.at[g, slot],
+            device_id={"seq": through},
+        )
+
+    def combined_copy(g):
+        return pltpu.make_async_remote_copy(
+            src_ref=comb_send.at[g],
+            dst_ref=comb_recv.at[g],
+            send_sem=comb_sem.at[0, g],
+            recv_sem=comb_sem.at[1, g],
+            device_id={"seq": served},
+        )
+
     def over_seq(action):
         def one(step, carry):
             action(lax.rem(me + step, n))
@@ -189,16 +269,39 @@
     for g in range(kv_local):
         cols = slice(g * HEAD_DIM, (g + 1) * HEAD_DIM)
 
+        if relay:
+
+            @pl.when(is_end)
+            def _(g=g, cols=cols):
+                full_send[g, :, :HEAD_DIM] = k_ref[:, cols]
+                full_send[g, :, HEAD_DIM:] = v_ref[:, cols]
+                full_copy(g).start()
+
         def send_kv(peer, g=g, cols=cols):
             second = half_tab[peer] == 1
             kv_send[g, peer, :, :HEAD_DIM] = jnp.where(second, k_ref[span:, cols], k_ref[:span, cols])
             kv_send[g, peer, :, HEAD_DIM:] = jnp.where(second, v_ref[span:, cols], v_ref[:span, cols])
-            kv_copy(peer, me, g).start()
+            only(jnp.logical_not(is_end & far(peer)), kv_copy(peer, me, g).start)
 
         over_seq(send_kv)
 
     fetches[2].wait()
     fetches[3].wait()
+    if relay:
+        for g in range(kv_local):
+
+            @pl.when(is_inner)
+            def _(g=g):
+                full_copy(g).wait_recv()
+                for at in range(4):
+                    second = sel_tab[at] == 1
+                    block = jnp.where(second, full_recv[g, span:], full_recv[g, :span])
+                    if at < 3:
+                        fwd_send[g, at] = block
+                        forward_copy(g, at).start()
+                    else:
+                        kv_recv[g][served] = block
+
     over_head(lambda peer: cot_copy(hd, peer).wait_recv())
 
     pair = 2
@@ -209,7 +312,11 @@
 
     for g in range(kv_local):
         cols = slice(g * HEAD_DIM, (g + 1) * HEAD_DIM)
-        over_seq(lambda peer, g=g: kv_copy(me, peer, g).wait_recv())
+        over_seq(
+            lambda peer, g=g: only(
+                jnp.logical_not(is_inner & (peer == served)), kv_copy(me, peer, g).wait_recv
+            )
+        )
 
         def attend(side, carry, g=g, cols=cols):
             base = pl.multiple_of(side * span, span)
@@ -279,10 +386,37 @@
                 found = jnp.where(hit, 1, found)
             part = parts[g, spot]
             g_send[g, peer] = jnp.where(found == 1, part, jnp.zeros_like(part))
-            grad_copy(peer, me, g).start()
+            through_other = peer_is_end(peer) & far(peer)
+            only(jnp.logical_not(through_other), grad_copy(peer, me, g).start)
+            if relay:
+                slot = jnp.where(is_inner, 0, jnp.where(lax.rem(peer, 2) == y, 1, 2))
+                here = is_inner & (peer == served)
+
+                @pl.when(through_other & jnp.logical_not(here))
+                def _():
+                    collect_copy(peer, slot, g).start()
 
         over_seq(send_grad)
         over_head(lambda peer, g=g: att_copy(peer, hd, g).start())
+
+    if relay:
+        for g in range(kv_local):
+
+            @pl.when(is_inner)
+            def _(g=g):
+                sums = [jnp.zeros((span, 2 * HEAD_DIM), jnp.float32)] * 2
+                for at in range(4):
+                    if at < 3:
+                        collect_copy(served, at, g).wait_recv()
+                        part = col_recv[g, at].astype(jnp.float32)
+                    else:
+                        part = g_send[g, served].astype(jnp.float32)
+                    second = sel_tab[at] == 1
+                    sums[0] = sums[0] + jnp.where(second, 0.0, part)
+                    sums[1] = sums[1] + jnp.where(second, part, 0.0)
+                for side in range(2):
+                    comb_send[g, side] = sums[side].astype(jnp.bfloat16)
+                combined_copy(g).start()
 
     leaving = [
         pltpu.make_async_copy(source, target, local_sem.at[at])
@@ -305,13 +439,24 @@
         cols = slice(g * HEAD_DIM, (g + 1) * HEAD_DIM)
 
         def add_grad(peer, g=g):
-            grad_copy(me, peer, g).wait_recv()
-            part = g_recv[g, peer].astype(jnp.float32)
-            second = half_tab[peer] == 1
-            own_acc[g, 0] += jnp.where(second, 0.0, part)
-            own_acc[g, 1] += jnp.where(second, part, 0.0)
+            def arrived():
+                grad_copy(me, peer, g).wait_recv()
+                part = g_recv[g, peer].astype(jnp.float32)
+                second = half_tab[peer] == 1
+                own_acc[g, 0] += jnp.where(second, 0.0, part)
+                own_acc[g, 1] += jnp.where(second, part, 0.0)
+
+            only(jnp.logical_not(is_end & far(peer)), arrived)
 
         over_seq(add_grad)
+        if relay:
+
+            @pl.when(is_end)
+            def _(g=g):
+                combined_copy(g).wait_recv()
+                for side in range(2):
+                    own_acc[g, side] += comb_recv[g, side].astype(jnp.float32)
+
         for side in range(2):
             here = slice(side * span, (side + 1) * span)
             kg_ref[here, cols] = own_acc[g, side, :, :HEAD_DIM].astype(jnp.bfloat16)
@@ -323,8 +468,28 @@
     for g in range(kv_local):
         over_head(lambda peer, g=g: att_copy(hd, peer, g).wait_recv())
         over_head(lambda peer, g=g: att_copy(peer, hd, g).wait_send())
-        over_seq(lambda peer, g=g: kv_copy(peer, me, g).wait_send())
-        over_seq(lambda peer, g=g: grad_copy(peer, me, g).wait_send())
+        over_seq(
+            lambda peer, g=g: only(
+                jnp.logical_not(is_end & far(peer)), kv_copy(peer, me, g).wait_send
+            )
+        )
+        over_seq(
+            lambda peer, g=g: only(
+                jnp.logical_not(is_inner & (peer == served)), grad_copy(peer, me, g).wait_send
+            )
+        )
+        if relay:
+
+            @pl.when(is_end)
+            def _(g=g):
+                full_copy(g).wait_send()
+
+            @pl.when(is_inner)
+            def _(g=g):
+                for at in range(3):
+                    forward_copy(g, at).wait_send()
+                combined_copy(g).wait_send()
+
     for copy in leaving:
         copy.wait()
 
@@ -398,6 +563,17 @@
             dma((kv_local, n)),
             dma((kv_local, n)),
             dma((kv_local, n)),
+            pltpu.SMEM((4,), jnp.int32),
+            pltpu.VMEM((kv_local, 2 * span, 2 * HEAD_DIM), bf16),
+            pltpu.VMEM((kv_local, 2 * span, 2 * HEAD_DIM), bf16),
+            pltpu.VMEM((kv_local, 3, span, 2 * HEAD_DIM), bf16),
+            pltpu.VMEM((kv_local, 3, span, 2 * HEAD_DIM), bf16),
+            pltpu.VMEM((kv_local, 2, span, 2 * HEAD_DIM), bf16),
+            pltpu.VMEM((kv_local, 2, span, 2 * HEAD_DIM), bf16),
+            dma((2, kv_local)),
+            dma((kv_local, 3)),
+            dma((kv_local, 3)),
+            dma((2, kv_local)),
         ],
         compiler_params=pltpu.CompilerParams(
             collective_id=0, has_side_effects=True, vmem_limit_bytes=VMEM_BYTES

time: 55.3 us -> 49.2 us (0.89)
  the two profiles are of different devices: /device:TPU:0 before, /device:TPU:26 now
where the time goes in v4:
time: 49.2 us; the launch traced here: 49 us
  Pallas kernels  48.3 us (98%)
  between operations  0.64 us (1%)
    pallas_call x1, Pallas kernels, body(): pl.pallas_call(functools.partial(kernel, (n, heads, span, picks, kv_local...  46.2 us
    pallas_call x1, Pallas kernels, body(): pl.pallas_call(write_out, out_shape=[jax.ShapeDtypeStruct(item.shape, ite...  2.16 us

profile of v4, /device:TPU:26, one launch (start us, length us, event | category | flops | bytes accessed | tf_op | source)
XLA Modules:
  0.0 49.0 jit_solution(3221294457598067391)
XLA Ops:
  0.6 46.2 %shard_map.93 = (bf16[64,4096]{1,0:T(8,128)(2,1)}, bf16[256,1024]{1,0:T(8,128)(2,1)}, bf16[256,256]{1,0:T(8,128)(2,1)}, bf16[256,256]{1,0:T(8,128)(2,1)}) custom-call(s32[16]{0:T(128)} %place_ref.1, s32[3,16]{1,0:T(4,128)} %bitcast.1, bf16[256,1024]{1,0:T(8,128)(2,1)} %q_in.1, bf16[256,256]{1,0:T(8,128)(2,1)} %k_in.1, bf16[256,256]{1,0:T(8,128)(2,1)} %v_in.1, ...), custom_call_target="tpu_custom_call" | custom-call | flops 1610612736 | bytes 2097152 | tf_op jit(solution)/shard_map/pallas_call | solution.py:529
  46.8 2.2 %shard_map.94 = (bf16[64,4096]{1,0:T(8,128)(2,1)}, bf16[256,1024]{1,0:T(8,128)(2,1)}, bf16[256,256]{1,0:T(8,128)(2,1)}, bf16[256,256]{1,0:T(8,128)(2,1)}) custom-call(bf16[64,4096]{1,0:T(8,128)(2,1)} %get-tuple-element.8.refs_0_, bf16[256,1024]{1,0:T(8,128)(2,1)} %get-tuple-element.9.refs_1_, bf16[256,256]{1,0:T(8,128)(2,1)} %get-tuple-element.10.refs_2_, ...), custom_call_target="tpu_custom_call" | custom-call | tf_op jit(solution)/shard_map/pallas_call | solution.py:586

commit v5 on v4

--- a/solution.py
+++ b/solution.py
@@ -266,32 +266,37 @@
     fetches[0].wait()
     fetches[1].wait()
 
-    for g in range(kv_local):
+    def send_keys(g):
         cols = slice(g * HEAD_DIM, (g + 1) * HEAD_DIM)
-
         if relay:
 
             @pl.when(is_end)
-            def _(g=g, cols=cols):
+            def _():
                 full_send[g, :, :HEAD_DIM] = k_ref[:, cols]
                 full_send[g, :, HEAD_DIM:] = v_ref[:, cols]
+                if g > 0:
+                    full_copy(g - 1).wait_send()
                 full_copy(g).start()
 
-        def send_kv(peer, g=g, cols=cols):
+        def send_kv(peer):
             second = half_tab[peer] == 1
             kv_send[g, peer, :, :HEAD_DIM] = jnp.where(second, k_ref[span:, cols], k_ref[:span, cols])
             kv_send[g, peer, :, HEAD_DIM:] = jnp.where(second, v_ref[span:, cols], v_ref[:span, cols])
-            only(jnp.logical_not(is_end & far(peer)), kv_copy(peer, me, g).start)
+
+            def go():
+                if g > 0:
+                    kv_copy(peer, me, g - 1).wait_send()
+                kv_copy(peer, me, g).start()
+
+            only(jnp.logical_not(is_end & far(peer)), go)
 
         over_seq(send_kv)
 
-    fetches[2].wait()
-    fetches[3].wait()
-    if relay:
-        for g in range(kv_local):
+    def relay_keys(g):
+        if relay:
 
             @pl.when(is_inner)
-            def _(g=g):
+            def _():
                 full_copy(g).wait_recv()
                 for at in range(4):
                     second = sel_tab[at] == 1
@@ -302,6 +307,12 @@
                     else:
                         kv_recv[g][served] = block
 
+    send_keys(0)
+    relay_keys(0)
+    for g in range(1, kv_local):
+        send_keys(g)
+    fetches[2].wait()
+    fetches[3].wait()
     over_head(lambda peer: cot_copy(hd, peer).wait_recv())
 
     pair = 2
@@ -312,6 +323,8 @@
 
     for g in range(kv_local):
         cols = slice(g * HEAD_DIM, (g + 1) * HEAD_DIM)
+        if g > 0:
+            relay_keys(g)
         over_seq(
             lambda peer, g=g: only(
                 jnp.logical_not(is_inner & (peer == served)), kv_copy(me, peer, g).wait_recv
@@ -464,25 +477,24 @@
 
     leaving[2].start()
     leaving[3].start()
+    last = kv_local - 1
+    over_seq(
+        lambda peer: only(
+            jnp.logical_not(is_end & far(peer)), kv_copy(peer, me, last).wait_send
+        )
+    )
+    if relay:
+        pl.when(is_end)(full_copy(last).wait_send)
     over_head(lambda peer: cot_copy(peer, hd).wait_send())
     for g in range(kv_local):
         over_head(lambda peer, g=g: att_copy(hd, peer, g).wait_recv())
         over_head(lambda peer, g=g: att_copy(peer, hd, g).wait_send())
         over_seq(
             lambda peer, g=g: only(
-                jnp.logical_not(is_end & far(peer)), kv_copy(peer, me, g).wait_send
-            )
-        )
-        over_seq(
-            lambda peer, g=g: only(
                 jnp.logical_not(is_inner & (peer == served)), grad_copy(peer, me, g).wait_send
             )
         )
         if relay:
-
-            @pl.when(is_end)
-            def _(g=g):
-                full_copy(g).wait_send()
 
             @pl.when(is_inner)
             def _(g=g):

time: 49.2 us -> 53 us (1.077)
  the two profiles are of different devices: /device:TPU:26 before, /device:TPU:0 now
where the time goes in v5:
time: 53 us; the launch traced here: 52.8 us
  Pallas kernels  52.1 us (98%)
  between operations  0.64 us (1%)
    pallas_call x1, Pallas kernels, body(): pl.pallas_call(functools.partial(kernel, (n, heads, span, picks, kv_local...  50 us
    pallas_call x1, Pallas kernels, body(): pl.pallas_call(write_out, out_shape=[jax.ShapeDtypeStruct(item.shape, ite...  2.16 us

profile of v5, /device:TPU:0, one launch (start us, length us, event | category | flops | bytes accessed | tf_op | source)
XLA Modules:
  0.0 52.8 jit_solution(6600057488200324456)
XLA Ops:
  0.6 50.0 %shard_map.93 = (bf16[64,4096]{1,0:T(8,128)(2,1)}, bf16[256,1024]{1,0:T(8,128)(2,1)}, bf16[256,256]{1,0:T(8,128)(2,1)}, bf16[256,256]{1,0:T(8,128)(2,1)}) custom-call(s32[16]{0:T(128)} %place_ref.1, s32[3,16]{1,0:T(4,128)} %bitcast.1, bf16[256,1024]{1,0:T(8,128)(2,1)} %q_in.1, bf16[256,256]{1,0:T(8,128)(2,1)} %k_in.1, bf16[256,256]{1,0:T(8,128)(2,1)} %v_in.1, ...), custom_call_target="tpu_custom_call" | custom-call | flops 1610612736 | bytes 2097152 | tf_op jit(solution)/shard_map/pallas_call | solution.py:541
  50.6 2.2 %shard_map.94 = (bf16[64,4096]{1,0:T(8,128)(2,1)}, bf16[256,1024]{1,0:T(8,128)(2,1)}, bf16[256,256]{1,0:T(8,128)(2,1)}, bf16[256,256]{1,0:T(8,128)(2,1)}) custom-call(bf16[64,4096]{1,0:T(8,128)(2,1)} %get-tuple-element.8.refs_0_, bf16[256,1024]{1,0:T(8,128)(2,1)} %get-tuple-element.9.refs_1_, bf16[256,256]{1,0:T(8,128)(2,1)} %get-tuple-element.10.refs_2_, ...), custom_call_target="tpu_custom_call" | custom-call | tf_op jit(solution)/shard_map/pallas_call | solution.py:598

commit v6 on v4

--- a/solution.py
+++ b/solution.py
@@ -266,32 +266,30 @@
     fetches[0].wait()
     fetches[1].wait()
 
-    for g in range(kv_local):
+    def send_keys(g):
         cols = slice(g * HEAD_DIM, (g + 1) * HEAD_DIM)
-
         if relay:
 
             @pl.when(is_end)
-            def _(g=g, cols=cols):
+            def _():
                 full_send[g, :, :HEAD_DIM] = k_ref[:, cols]
                 full_send[g, :, HEAD_DIM:] = v_ref[:, cols]
                 full_copy(g).start()
 
-        def send_kv(peer, g=g, cols=cols):
+        def send_kv(peer):
             second = half_tab[peer] == 1
             kv_send[g, peer, :, :HEAD_DIM] = jnp.where(second, k_ref[span:, cols], k_ref[:span, cols])
             kv_send[g, peer, :, HEAD_DIM:] = jnp.where(second, v_ref[span:, cols], v_ref[:span, cols])
+
             only(jnp.logical_not(is_end & far(peer)), kv_copy(peer, me, g).start)
 
         over_seq(send_kv)
 
-    fetches[2].wait()
-    fetches[3].wait()
-    if relay:
-        for g in range(kv_local):
+    def relay_keys(g):
+        if relay:
 
             @pl.when(is_inner)
-            def _(g=g):
+            def _():
                 full_copy(g).wait_recv()
                 for at in range(4):
                     second = sel_tab[at] == 1
@@ -302,6 +300,11 @@
                     else:
                         kv_recv[g][served] = block
 
+    for g in range(kv_local):
+        send_keys(g)
+    relay_keys(0)
+    fetches[2].wait()
+    fetches[3].wait()
     over_head(lambda peer: cot_copy(hd, peer).wait_recv())
 
     pair = 2
@@ -312,6 +315,8 @@
 
     for g in range(kv_local):
         cols = slice(g * HEAD_DIM, (g + 1) * HEAD_DIM)
+        if g > 0:
+            relay_keys(g)
         over_seq(
             lambda peer, g=g: only(
                 jnp.logical_not(is_inner & (peer == served)), kv_copy(me, peer, g).wait_recv
@@ -377,7 +382,7 @@
 
         lax.fori_loop(0, 2, attend, 0)
 
-        def send_grad(peer, g=g):
+        def stage_grad(peer, g=g):
             spot = jnp.int32(0)
             found = jnp.int32(0)
             for at in range(2 * picks):
@@ -386,17 +391,27 @@
                 found = jnp.where(hit, 1, found)
             part = parts[g, spot]
             g_send[g, peer] = jnp.where(found == 1, part, jnp.zeros_like(part))
-            through_other = peer_is_end(peer) & far(peer)
-            only(jnp.logical_not(through_other), grad_copy(peer, me, g).start)
-            if relay:
+
+        def send_through(peer, g=g):
+            @pl.when(peer_is_end(peer) & far(peer))
+            def _():
+                stage_grad(peer)
                 slot = jnp.where(is_inner, 0, jnp.where(lax.rem(peer, 2) == y, 1, 2))
-                here = is_inner & (peer == served)
-
-                @pl.when(through_other & jnp.logical_not(here))
+
+                @pl.when(jnp.logical_not(is_inner & (peer == served)))
                 def _():
                     collect_copy(peer, slot, g).start()
 
-        over_seq(send_grad)
+        def send_direct(peer, g=g):
+            def go():
+                stage_grad(peer)
+                grad_copy(peer, me, g).start()
+
+            only(jnp.logical_not(peer_is_end(peer) & far(peer)), go)
+
+        if relay:
+            over_seq(send_through)
+        over_seq(send_direct)
         over_head(lambda peer, g=g: att_copy(peer, hd, g).start())
 
     if relay:
@@ -480,9 +495,7 @@
         )
         if relay:
 
-            @pl.when(is_end)
-            def _(g=g):
-                full_copy(g).wait_send()
+            pl.when(is_end)(full_copy(g).wait_send)
 
             @pl.when(is_inner)
             def _(g=g):

time: 49.2 us -> 54.7 us (1.11)
  Pallas kernels: 48.3 us -> 53.9 us
    pallas_call x1, Pallas kernels: 46.2 us -> 51.8 us  [body(): pl.pallas_call(functools.partial(kernel, (n, heads, span, picks, kv_local...]
where the time goes in v6:
time: 54.7 us; the launch traced here: 54.6 us
  Pallas kernels  53.9 us (99%)
  between operations  0.64 us (1%)
    pallas_call x1, Pallas kernels, body(): pl.pallas_call(functools.partial(kernel, (n, heads, span, picks, kv_local...  51.8 us
    pallas_call x1, Pallas kernels, body(): pl.pallas_call(write_out, out_shape=[jax.ShapeDtypeStruct(item.shape, ite...  2.16 us

profile of v6, /device:TPU:26, one launch (start us, length us, event | category | flops | bytes accessed | tf_op | source)
XLA Modules:
  0.0 54.6 jit_solution(18331633659292457325)
XLA Ops:
  0.6 51.8 %shard_map.93 = (bf16[64,4096]{1,0:T(8,128)(2,1)}, bf16[256,1024]{1,0:T(8,128)(2,1)}, bf16[256,256]{1,0:T(8,128)(2,1)}, bf16[256,256]{1,0:T(8,128)(2,1)}) custom-call(s32[16]{0:T(128)} %place_ref.1, s32[3,16]{1,0:T(4,128)} %bitcast.1, bf16[256,1024]{1,0:T(8,128)(2,1)} %q_in.1, bf16[256,256]{1,0:T(8,128)(2,1)} %k_in.1, bf16[256,256]{1,0:T(8,128)(2,1)} %v_in.1, ...), custom_call_target="tpu_custom_call" | custom-call | flops 1610612736 | bytes 2097152 | tf_op jit(solution)/shard_map/pallas_call | solution.py:542
  52.4 2.2 %shard_map.94 = (bf16[64,4096]{1,0:T(8,128)(2,1)}, bf16[256,1024]{1,0:T(8,128)(2,1)}, bf16[256,256]{1,0:T(8,128)(2,1)}, bf16[256,256]{1,0:T(8,128)(2,1)}) custom-call(bf16[64,4096]{1,0:T(8,128)(2,1)} %get-tuple-element.8.refs_0_, bf16[256,1024]{1,0:T(8,128)(2,1)} %get-tuple-element.9.refs_1_, bf16[256,256]{1,0:T(8,128)(2,1)} %get-tuple-element.10.refs_2_, ...), custom_call_target="tpu_custom_call" | custom-call | tf_op jit(solution)/shard_map/pallas_call | solution.py:599

commit v7 on v6

--- a/solution.py
+++ b/solution.py
@@ -266,7 +266,7 @@
     fetches[0].wait()
     fetches[1].wait()
 
-    def send_keys(g):
+    def send_full(g):
         cols = slice(g * HEAD_DIM, (g + 1) * HEAD_DIM)
         if relay:
 
@@ -275,6 +275,9 @@
                 full_send[g, :, :HEAD_DIM] = k_ref[:, cols]
                 full_send[g, :, HEAD_DIM:] = v_ref[:, cols]
                 full_copy(g).start()
+
+    def send_keys(g):
+        cols = slice(g * HEAD_DIM, (g + 1) * HEAD_DIM)
 
         def send_kv(peer):
             second = half_tab[peer] == 1
@@ -301,8 +304,11 @@
                         kv_recv[g][served] = block
 
     for g in range(kv_local):
+        send_full(g)
+    for g in range(kv_local):
         send_keys(g)
-    relay_keys(0)
+    for g in range(kv_local):
+        relay_keys(g)
     fetches[2].wait()
     fetches[3].wait()
     over_head(lambda peer: cot_copy(hd, peer).wait_recv())
@@ -315,8 +321,6 @@
 
     for g in range(kv_local):
         cols = slice(g * HEAD_DIM, (g + 1) * HEAD_DIM)
-        if g > 0:
-            relay_keys(g)
         over_seq(
             lambda peer, g=g: only(
                 jnp.logical_not(is_inner & (peer == served)), kv_copy(me, peer, g).wait_recv

time: 54.7 us -> 48 us (0.88)
  the two profiles are of different devices: /device:TPU:26 before, /device:TPU:0 now
where the time goes in v7:
time: 48 us; the launch traced here: 47.8 us
  Pallas kernels  47.2 us (98%)
  between operations  0.64 us (1%)
    pallas_call x1, Pallas kernels, body(): pl.pallas_call(functools.partial(kernel, (n, heads, span, picks, kv_local...  45.1 us
    pallas_call x1, Pallas kernels, body(): pl.pallas_call(write_out, out_shape=[jax.ShapeDtypeStruct(item.shape, ite...  2.16 us

profile of v7, /device:TPU:0, one launch (start us, length us, event | category | flops | bytes accessed | tf_op | source)
XLA Modules:
  0.0 47.8 jit_solution(15177155172550371726)
XLA Ops:
  0.6 45.1 %shard_map.93 = (bf16[64,4096]{1,0:T(8,128)(2,1)}, bf16[256,1024]{1,0:T(8,128)(2,1)}, bf16[256,256]{1,0:T(8,128)(2,1)}, bf16[256,256]{1,0:T(8,128)(2,1)}) custom-call(s32[16]{0:T(128)} %place_ref.1, s32[3,16]{1,0:T(4,128)} %bitcast.1, bf16[256,1024]{1,0:T(8,128)(2,1)} %q_in.1, bf16[256,256]{1,0:T(8,128)(2,1)} %k_in.1, bf16[256,256]{1,0:T(8,128)(2,1)} %v_in.1, ...), custom_call_target="tpu_custom_call" | custom-call | flops 1610612736 | bytes 2097152 | tf_op jit(solution)/shard_map/pallas_call | solution.py:546
  45.7 2.2 %shard_map.94 = (bf16[64,4096]{1,0:T(8,128)(2,1)}, bf16[256,1024]{1,0:T(8,128)(2,1)}, bf16[256,256]{1,0:T(8,128)(2,1)}, bf16[256,256]{1,0:T(8,128)(2,1)}) custom-call(bf16[64,4096]{1,0:T(8,128)(2,1)} %get-tuple-element.8.refs_0_, bf16[256,1024]{1,0:T(8,128)(2,1)} %get-tuple-element.9.refs_1_, bf16[256,256]{1,0:T(8,128)(2,1)} %get-tuple-element.10.refs_2_, ...), custom_call_target="tpu_custom_call" | custom-call | tf_op jit(solution)/shard_map/pallas_call | solution.py:603

commit v8 on v7

--- a/solution.py
+++ b/solution.py
@@ -10,6 +10,7 @@
 
 HEAD_DIM = 128
 HIDDEN = -1e30
+LOG2_E = math.log2(math.e)
 VMEM_BYTES = 64 * 1024 * 1024
 
 
@@ -286,7 +287,18 @@
 
             only(jnp.logical_not(is_end & far(peer)), kv_copy(peer, me, g).start)
 
-        over_seq(send_kv)
+        def over_seq_back():
+            def one(step, carry):
+                send_kv(lax.rem(me + n - step, n))
+                return carry
+
+            lax.fori_loop(1, n, one, 0)
+
+        if relay:
+            pl.when(z == 1)(over_seq_back)
+            pl.when(z != 1)(lambda: over_seq(send_kv))
+        else:
+            over_seq(send_kv)
 
     def relay_keys(g):
         if relay:
@@ -349,24 +361,30 @@
                 ]
                 query = jnp.concatenate([q_ref[here, spot] for spot in spots], axis=0)
                 grad = jnp.concatenate([do_buf[here, spot] for spot in spots], axis=0)
-                scores = dot(keys, query, 1, 1) * scale
-                masked = [jnp.where(causal, scores[:span], HIDDEN)]
+                scores = dot(keys, query, 1, 1)
+                pieces = [
+                    scores[at * span : (at + 1) * span] for at in range(picks + 1)
+                ]
+                pieces[0] = jnp.where(causal, pieces[0], HIDDEN)
+                tops = [jnp.max(piece, axis=0, keepdims=True) for piece in pieces]
+                top = tops[0]
                 for pick in range(picks):
-                    piece = scores[(pick + 1) * span : (pick + 2) * span]
-                    masked.append(jnp.where(valid[pick], piece, HIDDEN))
-                scores = jnp.concatenate(masked, axis=0)
-                top = jnp.max(scores, axis=0, keepdims=True)
-                probs = jnp.exp(scores - top)
+                    top = jnp.maximum(top, jnp.where(valid[pick], tops[pick + 1], HIDDEN))
+                probs = [jnp.exp2((pieces[0] - top) * (scale * LOG2_E))]
+                for pick in range(picks):
+                    above = jnp.where(valid[pick], top, -HIDDEN)
+                    probs.append(jnp.exp2((pieces[pick + 1] - above) * (scale * LOG2_E)))
+                probs = jnp.concatenate(probs, axis=0)
                 total = jnp.sum(probs, axis=0, keepdims=True)
                 probs = probs * (1.0 / total)
                 weights = probs.astype(jnp.bfloat16)
                 attended = dot(values, weights, 0, 0)
                 slopes = dot(values, grad, 1, 1)
                 delta = jnp.sum(probs * slopes, axis=0, keepdims=True)
-                dscores = (probs * ((slopes - delta) * scale)).astype(jnp.bfloat16)
+                dscores = (probs * (slopes - delta)).astype(jnp.bfloat16)
                 query_grad = dot(keys, dscores, 0, 0)
                 attended = attended.T.astype(jnp.bfloat16)
-                query_grad = query_grad.T.astype(jnp.bfloat16)
+                query_grad = (query_grad * scale).T.astype(jnp.bfloat16)
                 for at in range(pair):
                     att_buf[here, spots[at]] = attended[at * span : (at + 1) * span]
                     qg_ref[here, spots[at]] = query_grad[at * span : (at + 1) * span]
@@ -376,6 +394,7 @@
                     key_sum, value_sum = key_part, value_part
                 else:
                     key_sum, value_sum = key_sum + key_part, value_sum + value_part
+            key_sum = key_sum * scale
             own_acc[g, side, :, :HEAD_DIM] = key_sum[:span]
             own_acc[g, side, :, HEAD_DIM:] = value_sum[:span]
             for pick in range(picks):

time: 48 us -> 48.6 us (1.012)
  Pallas kernels: 47.2 us -> 47.7 us
    pallas_call x1, Pallas kernels: 45.1 us -> 45.6 us  [body(): pl.pallas_call(functools.partial(kernel, (n, heads, span, picks, kv_local...]
where the time goes in v8:
time: 48.6 us; the launch traced here: 48.4 us
  Pallas kernels  47.7 us (98%)
  between operations  0.64 us (1%)
    pallas_call x1, Pallas kernels, body(): pl.pallas_call(functools.partial(kernel, (n, heads, span, picks, kv_local...  45.6 us
    pallas_call x1, Pallas kernels, body(): pl.pallas_call(write_out, out_shape=[jax.ShapeDtypeStruct(item.shape, ite...  2.16 us

profile of v8, /device:TPU:0, one launch (start us, length us, event | category | flops | bytes accessed | tf_op | source)
XLA Modules:
  0.0 48.4 jit_solution(8147997541247409203)
XLA Ops:
  0.6 45.6 %shard_map.93 = (bf16[64,4096]{1,0:T(8,128)(2,1)}, bf16[256,1024]{1,0:T(8,128)(2,1)}, bf16[256,256]{1,0:T(8,128)(2,1)}, bf16[256,256]{1,0:T(8,128)(2,1)}) custom-call(s32[16]{0:T(128)} %place_ref.1, s32[3,16]{1,0:T(4,128)} %bitcast.1, bf16[256,1024]{1,0:T(8,128)(2,1)} %q_in.1, bf16[256,256]{1,0:T(8,128)(2,1)} %k_in.1, bf16[256,256]{1,0:T(8,128)(2,1)} %v_in.1, ...), custom_call_target="tpu_custom_call" | custom-call | flops 1610612736 | bytes 2097152 | tf_op jit(solution)/shard_map/pallas_call | solution.py:565
  46.2 2.2 %shard_map.94 = (bf16[64,4096]{1,0:T(8,128)(2,1)}, bf16[256,1024]{1,0:T(8,128)(2,1)}, bf16[256,256]{1,0:T(8,128)(2,1)}, bf16[256,256]{1,0:T(8,128)(2,1)}) custom-call(bf16[64,4096]{1,0:T(8,128)(2,1)} %get-tuple-element.8.refs_0_, bf16[256,1024]{1,0:T(8,128)(2,1)} %get-tuple-element.9.refs_1_, bf16[256,256]{1,0:T(8,128)(2,1)} %get-tuple-element.10.refs_2_, ...), custom_call_target="tpu_custom_call" | custom-call | tf_op jit(solution)/shard_map/pallas_call | solution.py:622

commit v9 on v8

--- a/solution.py
+++ b/solution.py
@@ -10,6 +10,7 @@
 
 HEAD_DIM = 128
 HIDDEN = -1e30
+CHUNKS = 4
 LOG2_E = math.log2(math.e)
 VMEM_BYTES = 64 * 1024 * 1024
 
@@ -287,18 +288,7 @@
 
             only(jnp.logical_not(is_end & far(peer)), kv_copy(peer, me, g).start)
 
-        def over_seq_back():
-            def one(step, carry):
-                send_kv(lax.rem(me + n - step, n))
-                return carry
-
-            lax.fori_loop(1, n, one, 0)
-
-        if relay:
-            pl.when(z == 1)(over_seq_back)
-            pl.when(z != 1)(lambda: over_seq(send_kv))
-        else:
-            over_seq(send_kv)
+        over_seq(send_kv)
 
     def relay_keys(g):
         if relay:
@@ -532,19 +522,24 @@
 
 def write_out(*refs):
     sources, targets, stages, sems = refs[:4], refs[4:8], refs[8:12], refs[12]
-    arrive = [
-        pltpu.make_async_copy(source, stage, sems.at[0, at])
-        for at, (source, stage) in enumerate(zip(sources, stages))
-    ]
-    leave = [
-        pltpu.make_async_copy(stage, target, sems.at[1, at])
-        for at, (stage, target) in enumerate(zip(stages, targets))
-    ]
+    arrive = []
+    leave = []
+    for source, target, stage in zip(sources, targets, stages):
+        piece = source.shape[0] // CHUNKS
+        for at in range(CHUNKS):
+            rows = slice(at * piece, (at + 1) * piece)
+            spot = len(arrive)
+            arrive.append(
+                pltpu.make_async_copy(source.at[rows], stage.at[rows], sems.at[0, spot])
+            )
+            leave.append(
+                pltpu.make_async_copy(stage.at[rows], target.at[rows], sems.at[1, spot])
+            )
     for copy in arrive:
         copy.start()
-    for at in range(4):
-        arrive[at].wait()
-        leave[at].start()
+    for came, goes in zip(arrive, leave):
+        came.wait()
+        goes.start()
     for copy in leave:
         copy.wait()
 
@@ -625,7 +620,7 @@
             in_specs=[hbm] * 4,
             out_specs=[hbm] * 4,
             scratch_shapes=[pltpu.VMEM(item.shape, item.dtype) for item in results]
-            + [dma((2, 4))],
+            + [dma((2, 4 * CHUNKS))],
             compiler_params=pltpu.CompilerParams(vmem_limit_bytes=VMEM_BYTES),
         )(*results)
     )

time: 48.6 us -> 48.1 us (0.990)
    pallas_call x1, Pallas kernels: 45.6 us -> 44.9 us  [body(): pl.pallas_call(functools.partial(kernel, (n, heads, span, picks, kv_local...]
where the time goes in v9:
time: 48.1 us; the launch traced here: 47.9 us
  Pallas kernels  47.3 us (98%)
  between operations  0.64 us (1%)
    pallas_call x1, Pallas kernels, body(): pl.pallas_call(functools.partial(kernel, (n, heads, span, picks, kv_local...  44.9 us
    pallas_call x1, Pallas kernels, body(): pl.pallas_call(write_out, out_shape=[jax.ShapeDtypeStruct(item.shape, ite...  2.31 us

profile of v9, /device:TPU:0, one launch (start us, length us, event | category | flops | bytes accessed | tf_op | source)
XLA Modules:
  0.0 47.9 jit_solution(16745560978764074468)
XLA Ops:
  0.6 44.9 %shard_map.93 = (bf16[64,4096]{1,0:T(8,128)(2,1)}, bf16[256,1024]{1,0:T(8,128)(2,1)}, bf16[256,256]{1,0:T(8,128)(2,1)}, bf16[256,256]{1,0:T(8,128)(2,1)}) custom-call(s32[16]{0:T(128)} %place_ref.1, s32[3,16]{1,0:T(4,128)} %bitcast.1, bf16[256,1024]{1,0:T(8,128)(2,1)} %q_in.1, bf16[256,256]{1,0:T(8,128)(2,1)} %k_in.1, bf16[256,256]{1,0:T(8,128)(2,1)} %v_in.1, ...), custom_call_target="tpu_custom_call" | custom-call | flops 1610612736 | bytes 2097152 | tf_op jit(solution)/shard_map/pallas_call | solution.py:560
  45.6 2.3 %shard_map.94 = (bf16[64,4096]{1,0:T(8,128)(2,1)}, bf16[256,1024]{1,0:T(8,128)(2,1)}, bf16[256,256]{1,0:T(8,128)(2,1)}, bf16[256,256]{1,0:T(8,128)(2,1)}) custom-call(bf16[64,4096]{1,0:T(8,128)(2,1)} %get-tuple-element.8.refs_0_, bf16[256,1024]{1,0:T(8,128)(2,1)} %get-tuple-element.9.refs_1_, bf16[256,256]{1,0:T(8,128)(2,1)} %get-tuple-element.10.refs_2_, ...), custom_call_target="tpu_custom_call" | custom-call | tf_op jit(solution)/shard_map/pallas_call | solution.py:617

commit v10 on v9

--- a/solution.py
+++ b/solution.py
@@ -143,34 +143,6 @@
 
     lax.fori_loop(0, n, fill_half, 0)
 
-    if relay:
-        end_second = place_ref[2 * served + 1]
-        for at, who in enumerate(helped + (me,)):
-            wants = jnp.int32(0)
-            for side in range(2):
-                block = place_ref[2 * who + side]
-                for pick in range(picks):
-                    wants = jnp.where(lists_ref[pick, block] == end_second, 1, wants)
-            sel_tab[at] = wants
-
-    spare = lax.rem(me + 1, n)
-    for side in range(2):
-        own = place_ref[2 * me + side]
-        blocks = [lists_ref[pick, own] for pick in range(picks)]
-        for pick in range(picks):
-            block = blocks[pick]
-            valid = jnp.where(block != own, 1, 0)
-            for before in range(pick):
-                valid = jnp.where(block == blocks[before], 0, valid)
-
-            def find(at, owner, block=block):
-                hit = (place_ref[2 * at] == block) | (place_ref[2 * at + 1] == block)
-                return jnp.where(hit, at, owner)
-
-            owner = lax.fori_loop(0, n, find, jnp.int32(0))
-            owner_tab[side * picks + pick] = jnp.where(valid == 1, owner, spare)
-            valid_tab[side * picks + pick] = valid
-
     pl.semaphore_wait(barrier, n - 1 + heads - 1)
 
     def cot_copy(peer, slot):
@@ -309,6 +281,35 @@
         send_full(g)
     for g in range(kv_local):
         send_keys(g)
+
+    if relay:
+        end_second = place_ref[2 * served + 1]
+        for at, who in enumerate(helped + (me,)):
+            wants = jnp.int32(0)
+            for side in range(2):
+                block = place_ref[2 * who + side]
+                for pick in range(picks):
+                    wants = jnp.where(lists_ref[pick, block] == end_second, 1, wants)
+            sel_tab[at] = wants
+
+    spare = lax.rem(me + 1, n)
+    for side in range(2):
+        own = place_ref[2 * me + side]
+        blocks = [lists_ref[pick, own] for pick in range(picks)]
+        for pick in range(picks):
+            block = blocks[pick]
+            valid = jnp.where(block != own, 1, 0)
+            for before in range(pick):
+                valid = jnp.where(block == blocks[before], 0, valid)
+
+            def find(at, owner, block=block):
+                hit = (place_ref[2 * at] == block) | (place_ref[2 * at + 1] == block)
+                return jnp.where(hit, at, owner)
+
+            owner = lax.fori_loop(0, n, find, jnp.int32(0))
+            owner_tab[side * picks + pick] = jnp.where(valid == 1, owner, spare)
+            valid_tab[side * picks + pick] = valid
+
     for g in range(kv_local):
         relay_keys(g)
     fetches[2].wait()
@@ -393,7 +394,8 @@
                 parts[g, side * picks + pick, :, HEAD_DIM:] = value_sum[piece].astype(jnp.bfloat16)
             return carry
 
-        lax.fori_loop(0, 2, attend, 0)
+        for side in range(2):
+            attend(side, 0)
 
         def stage_grad(peer, g=g):
             spot = jnp.int32(0)

time: 48.1 us -> 47.9 us (level)
  no operation moved by 1% of the time
where the time goes in v10:
time: 47.9 us; the launch traced here: 47.8 us
  Pallas kernels  47.1 us (98%)
  between operations  0.64 us (1%)
    pallas_call x1, Pallas kernels, body(): pl.pallas_call(functools.partial(kernel, (n, heads, span, picks, kv_local...  44.8 us
    pallas_call x1, Pallas kernels, body(): pl.pallas_call(write_out, out_shape=[jax.ShapeDtypeStruct(item.shape, ite...  2.31 us

profile of v10, /device:TPU:0, one launch (start us, length us, event | category | flops | bytes accessed | tf_op | source)
XLA Modules:
  0.0 47.8 jit_solution(9146946678189748546)
XLA Ops:
  0.6 44.8 %shard_map.93 = (bf16[64,4096]{1,0:T(8,128)(2,1)}, bf16[256,1024]{1,0:T(8,128)(2,1)}, bf16[256,256]{1,0:T(8,128)(2,1)}, bf16[256,256]{1,0:T(8,128)(2,1)}) custom-call(s32[16]{0:T(128)} %place_ref.1, s32[3,16]{1,0:T(4,128)} %bitcast.1, bf16[256,1024]{1,0:T(8,128)(2,1)} %q_in.1, bf16[256,256]{1,0:T(8,128)(2,1)} %k_in.1, bf16[256,256]{1,0:T(8,128)(2,1)} %v_in.1, ...), custom_call_target="tpu_custom_call" | custom-call | flops 1610612736 | bytes 2097152 | tf_op jit(solution)/shard_map/pallas_call | solution.py:562
  45.5 2.3 %shard_map.94 = (bf16[64,4096]{1,0:T(8,128)(2,1)}, bf16[256,1024]{1,0:T(8,128)(2,1)}, bf16[256,256]{1,0:T(8,128)(2,1)}, bf16[256,256]{1,0:T(8,128)(2,1)}) custom-call(bf16[64,4096]{1,0:T(8,128)(2,1)} %get-tuple-element.8.refs_0_, bf16[256,1024]{1,0:T(8,128)(2,1)} %get-tuple-element.9.refs_1_, bf16[256,256]{1,0:T(8,128)(2,1)} %get-tuple-element.10.refs_2_, ...), custom_call_target="tpu_custom_call" | custom-call | tf_op jit(solution)/shard_map/pallas_call | solution.py:619

commit v11 on v10

--- a/solution.py
+++ b/solution.py
@@ -394,8 +394,7 @@
                 parts[g, side * picks + pick, :, HEAD_DIM:] = value_sum[piece].astype(jnp.bfloat16)
             return carry
 
-        for side in range(2):
-            attend(side, 0)
+        lax.fori_loop(0, 2, attend, 0)
 
         def stage_grad(peer, g=g):
             spot = jnp.int32(0)

time: 47.9 us -> 48.1 us (level)
  no operation moved by 1% of the time
where the time goes in v11:
time: 48.1 us; the launch traced here: 47.9 us
  Pallas kernels  47.3 us (98%)
  between operations  0.64 us (1%)
    pallas_call x1, Pallas kernels, body(): pl.pallas_call(functools.partial(kernel, (n, heads, span, picks, kv_local...  44.9 us
    pallas_call x1, Pallas kernels, body(): pl.pallas_call(write_out, out_shape=[jax.ShapeDtypeStruct(item.shape, ite...  2.31 us

profile of v11, /device:TPU:0, one launch (start us, length us, event | category | flops | bytes accessed | tf_op | source)
XLA Modules:
  0.0 47.9 jit_solution(2454456519559490208)
XLA Ops:
  0.6 44.9 %shard_map.93 = (bf16[64,4096]{1,0:T(8,128)(2,1)}, bf16[256,1024]{1,0:T(8,128)(2,1)}, bf16[256,256]{1,0:T(8,128)(2,1)}, bf16[256,256]{1,0:T(8,128)(2,1)}) custom-call(s32[16]{0:T(128)} %place_ref.1, s32[3,16]{1,0:T(4,128)} %bitcast.1, bf16[256,1024]{1,0:T(8,128)(2,1)} %q_in.1, bf16[256,256]{1,0:T(8,128)(2,1)} %k_in.1, bf16[256,256]{1,0:T(8,128)(2,1)} %v_in.1, ...), custom_call_target="tpu_custom_call" | custom-call | flops 1610612736 | bytes 2097152 | tf_op jit(solution)/shard_map/pallas_call | solution.py:561
  45.6 2.3 %shard_map.94 = (bf16[64,4096]{1,0:T(8,128)(2,1)}, bf16[256,1024]{1,0:T(8,128)(2,1)}, bf16[256,256]{1,0:T(8,128)(2,1)}, bf16[256,256]{1,0:T(8,128)(2,1)}) custom-call(bf16[64,4096]{1,0:T(8,128)(2,1)} %get-tuple-element.8.refs_0_, bf16[256,1024]{1,0:T(8,128)(2,1)} %get-tuple-element.9.refs_1_, bf16[256,256]{1,0:T(8,128)(2,1)} %get-tuple-element.10.refs_2_, ...), custom_call_target="tpu_custom_call" | custom-call | tf_op jit(solution)/shard_map/pallas_call | solution.py:618
